TPU v7x, 256 devices: a whole 4x4x8 slice. The times are simulated.
256 devices in a mesh: blk: 32 (over y_hi, z, core), uly: 8 (over x, y_lo).
Axes of the slice: x: 4, y: 4 (y_hi: 2, y_lo: 2; y = y_hi * 2 + y_lo), z: 8, core: 2. Of those that a mesh axis runs over, the one named last changes fastest.
Arguments:
- block_in: bfloat16 [2, 64, 64, 3072], P(None, 'blk', 'uly'), may hold values from -6 to 6
- mod_shift: float32 [3072], replicated, may hold values from -3 to 3
- mod_scale: float32 [3072], replicated, may hold values from -0.5 to 0.8
- mod_gate: float32 [3072], replicated, may hold values from -6 to 6
- qkv_weight: bfloat16 [3, 3072, 3072], P(None, None, 'uly'), may hold values from -0.09021098 to 0.09021098
- q_gain: float32 [128], replicated, may hold values from 1.3 to 6.5
- k_gain: float32 [128], replicated, may hold values from 1.3 to 6.5
- out_weight: bfloat16 [3072, 3072], P('uly'), may hold values from -0.109375 to 0.109375
- final_shift: float32 [3072], replicated, may hold values from -3 to 3
- final_scale: float32 [3072], replicated, may hold values from -0.5 to 0.8
- final_weight: bfloat16 [3072, 64], replicated, may hold values from -0.109375 to 0.109375
- final_bias: float32 [64], replicated, may hold values from -3 to 3
- conv_weight: bfloat16 [3, 3, 3, 16, 512], replicated, may hold values from -0.3125 to 0.3125
- conv_bias: float32 [512], replicated, may hold values from -3 to 3
Outputs:
- block_out: bfloat16 [2, 64, 64, 3072], P(None, 'blk', 'uly')
- conv_out: bfloat16 [2, 128, 128, 512], P(None, 'blk', 'uly')
All inputs are finite; a program needn't handle non-finite values.
Results may differ from a plain program's by a relative error of at most 0.019.
Values may be sent and summed in bfloat16 or wider, within the bound.
No kernel may reach another device: no remote copies, remote signals or barrier semaphores. Data moves between devices by JAX's collectives and lax.ppermute only.
A program may use at most 192 MiB of HBM per device.

v0:
```python
import functools

import jax
import jax.numpy as jnp
import numpy as np
from jax import lax
from jax.experimental import pallas as pl
from jax.experimental.pallas import tpu as pltpu
from jax.sharding import PartitionSpec as P

HD = 128
RT = 16
RH = 56
Z = 8
X = 4
HEADS = 3
GROUP = HEADS * HD
WIDTH = 3072
LOCAL = 32
PAIR = 2 * LOCAL
TOKENS = X * PAIR
STATS = 16
HALF = WIDTH // 2
LEFT = 1280
RIGHT = WIDTH - LEFT
MINE = TOKENS // 2
ORDER = (0, 3, 1, 2)
SCALE2 = float(HD ** (-0.5) / np.log(2.0))
F32 = jnp.float32
BF16 = jnp.bfloat16


def params(mib=12):
    return pltpu.CompilerParams(vmem_limit_bytes=mib * 1024 * 1024)


def whole():
    return pl.BlockSpec(memory_space=pltpu.VMEM)


def full(shape):
    return pl.BlockSpec(shape, lambda *_: (0,) * len(shape))


def blk_pairs(dy, dz, dc):
    return [
        (y * 2 * Z + z * 2 + c, (y ^ dy) * 2 * Z + (z + dz) % Z * 2 + (c ^ dc))
        for y in range(2)
        for z in range(Z)
        for c in range(2)
    ]


def ring_pairs():
    return [
        (y * 2 * Z + z * 2 + c, y * 2 * Z + (z + 1 - 2 * c) % Z * 2 + c)
        for y in range(2)
        for z in range(Z)
        for c in range(2)
    ]


def uly_pairs(ex, ey):
    return [(x * 2 + y, (x ^ ex) * 2 + (y ^ ey)) for x in range(X) for y in range(2)]


def send_blk(value, dy=0, dz=0, dc=0):
    return lax.ppermute(value, "blk", blk_pairs(dy, dz, dc))


def send_ring(value):
    return lax.ppermute(value, "blk", ring_pairs())


def send_uly(value, ex=0, ey=0):
    return lax.ppermute(value, "uly", uly_pairs(ex, ey))


def spread_x(value):
    came = {ex: send_uly(value, ex=ex) for ex in (2, 3, 1)}
    return [came[ex] for ex in ORDER[1:]]


def send_both(value, dy, ex):
    count = X * 2
    pairs = [
        (b * count + u, to_b * count + to_u)
        for b, to_b in blk_pairs(dy, 0, 0)
        for u, to_u in uly_pairs(ex, 0)
    ]
    return lax.ppermute(value, ("blk", "uly"), pairs)


def normed(values):
    center = values - jnp.mean(values, axis=-1, keepdims=True)
    spread = jnp.mean(center * center, axis=-1, keepdims=True)
    return center * lax.rsqrt(spread + 1e-06)


def modulate_kernel(tokens, scale_shift, left, right):
    scale, shift = scale_shift[0:1, :], scale_shift[1:2, :]
    x_mod = (normed(tokens[...].astype(F32)) * (1.0 + scale) + shift).astype(BF16)
    left[...] = x_mod[:, :LEFT]
    right[...] = x_mod[:, LEFT:]


def modulate(tokens, scale, shift):
    return pl.pallas_call(
        modulate_kernel,
        out_shape=[
            jax.ShapeDtypeStruct((LOCAL, LEFT), BF16),
            jax.ShapeDtypeStruct((LOCAL, RIGHT), BF16),
        ],
        compiler_params=params(),
    )(tokens, jnp.stack([scale, shift]))


def fetch_kernel(weight, after, query, key_value, sems):
    copies = [
        pltpu.make_async_copy(weight.at[0], query, sems.at[0]),
        pltpu.make_async_copy(weight.at[pl.ds(1, 2)], key_value, sems.at[1]),
    ]
    for copy in copies:
        copy.start()
    for copy in copies:
        copy.wait()


def fetch(weight, after):
    return pl.pallas_call(
        fetch_kernel,
        in_specs=[pl.BlockSpec(memory_space=pl.ANY)] * 2,
        out_specs=[whole(), whole()],
        out_shape=[
            jax.ShapeDtypeStruct((WIDTH, GROUP), BF16),
            jax.ShapeDtypeStruct((2, WIDTH, GROUP), BF16),
        ],
        scratch_shapes=[pltpu.SemaphoreType.DMA((2,))],
        compiler_params=params(),
    )(weight, after)


def rope_tables():
    uly = lax.axis_index("uly")
    lane = np.arange(HD)
    section = np.where(lane < RT, 0, np.where(lane < RT + RH, 1, 2))
    start = np.array([0, RT, RT + RH])[section]
    length = np.array([RT, RH, RH])[section]
    half = length // 2
    upper = (lane - start) >= half
    index = jnp.asarray((lane - start) % half, F32)
    rates = 256.0 ** (-2.0 * index / jnp.asarray(length, F32))
    place = jnp.arange(TOKENS, dtype=jnp.int32)
    slot, dy, within = place // PAIR, place // LOCAL % 2, place % LOCAL
    ex = jnp.where(slot == 0, 0, (slot + 1) % 3 + 1)
    member = ((uly // 2) ^ ex) * 2 + ((uly % 2) ^ dy)
    frames_at = within // 16
    rows_at = lax.axis_index("blk") * 2 + within // 8 % 2
    columns_at = member * 8 + within % 8
    where = jnp.where(
        section[None, :] == 0,
        frames_at[:, None],
        jnp.where(section[None, :] == 1, rows_at[:, None], columns_at[:, None]),
    ).astype(F32)
    angles = where * rates[None, :]
    sign = jnp.asarray(np.where(upper, 1.0, -1.0), F32)
    return jnp.cos(angles), jnp.sin(angles) * sign[None, :]


def rope_partner(values):
    lane = lax.broadcasted_iota(jnp.int32, values.shape, 1)
    time_half, space_half = RT // 2, RH // 2
    first = jnp.where(
        lane < time_half,
        pltpu.roll(values, HD - time_half, axis=1),
        pltpu.roll(values, time_half, axis=1),
    )
    low = (lane < RT + space_half) | ((lane >= RT + RH) & (lane < RT + RH + space_half))
    rest = jnp.where(
        low, pltpu.roll(values, HD - space_half, axis=1), pltpu.roll(values, space_half, axis=1)
    )
    return jnp.where(lane < RT, first, rest)


def headed(mixed, gain, cosine, sine):
    out = []
    for head in range(HEADS):
        one = mixed[:, head * HD : (head + 1) * HD]
        one = one * lax.rsqrt(jnp.mean(one * one, axis=-1, keepdims=True) + 1e-06) * gain
        out.append((one * cosine + rope_partner(one) * sine).astype(BF16))
    return jnp.concatenate(out, axis=1)


def key_value_kernel(a0, a1, a2, a3, b0, b1, weight, gain, cosine, sine, out, gathered):
    for step, ref in enumerate((a0, a1, a2, a3)):
        gathered[step * PAIR : (step + 1) * PAIR, :LEFT] = ref[...]
        for side, other in enumerate((b0, b1)):
            start = step * PAIR + side * LOCAL
            gathered[start : start + LOCAL, LEFT:] = other[step * LOCAL : (step + 1) * LOCAL, :]
    keys = jnp.dot(gathered[...], weight[0], preferred_element_type=F32)
    out[0] = headed(keys, gain[...], cosine[...], sine[...])
    out[1] = jnp.dot(gathered[...], weight[1], preferred_element_type=F32).astype(BF16)


def project_key_value(pieces, weight, gain, cosine, sine):
    return pl.pallas_call(
        key_value_kernel,
        out_shape=[
            jax.ShapeDtypeStruct((2, TOKENS, GROUP), BF16),
            jax.ShapeDtypeStruct((TOKENS, WIDTH), BF16),
        ],
        compiler_params=params(),
    )(*pieces, weight, gain, cosine, sine)


def query_kernel(gathered, weight, gain, cosine, sine, out):
    mixed = jnp.dot(gathered[...], weight[...], preferred_element_type=F32)
    out[...] = headed(mixed, gain[...], cosine[...], sine[...])


def project_query(gathered, weight, gain, cosine, sine):
    return pl.pallas_call(
        query_kernel,
        out_shape=jax.ShapeDtypeStruct((TOKENS, GROUP), BF16),
        compiler_params=params(),
    )(gathered, weight, gain, cosine, sine)


def attend_items(items, blocks):
    scores = [
        [
            lax.dot_general(
                ref[0, :, lanes], query, (((1,), (1,)), ((), ())), preferred_element_type=F32
            )
            for ref in blocks
        ]
        for query, lanes, _ in items
    ]
    tops = [
        functools.reduce(jnp.maximum, [jnp.max(part, axis=0, keepdims=True) for part in score])
        for score in scores
    ]
    tops = [
        top if old is None else jnp.maximum(top, old[1]) for top, (_, _, old) in zip(tops, items)
    ]
    raised = [
        [jnp.exp2(part * SCALE2 - top * SCALE2) for part in score]
        for score, top in zip(scores, tops)
    ]
    results = []
    for part, top, (_, lanes, old) in zip(raised, tops, items):
        denominator = functools.reduce(
            jnp.add, [jnp.sum(one, axis=0, keepdims=True) for one in part]
        )
        numerator = functools.reduce(
            jnp.add,
            [
                lax.dot_general(
                    ref[1, :, lanes],
                    one.astype(BF16),
                    (((0,), (0,)), ((), ())),
                    preferred_element_type=F32,
                )
                for one, ref in zip(part, blocks)
            ],
        )
        if old is not None:
            fade = jnp.exp2((old[1] - top) * SCALE2)
            numerator = numerator + old[0] * fade
            denominator = denominator + old[2] * fade
        results.append((numerator, top, denominator))
    return results


def head_lanes(head):
    return slice(head * HD, (head + 1) * HD)


def old_state(total, stat, head):
    return (
        total[head_lanes(head), :],
        stat[head : head + 1, :],
        stat[HEADS + head : HEADS + head + 1, :],
    )


def attend_kernel(count, fresh, *refs):
    queries, blocks, refs = refs[0], refs[1 : 1 + count], refs[1 + count :]
    if not fresh:
        old_total, old_stat, refs = refs[0], refs[1], refs[2:]
    total, stat = refs
    items = [
        (
            queries[:, head_lanes(head)],
            head_lanes(head),
            None if fresh else old_state(old_total, old_stat, head),
        )
        for head in range(HEADS)
    ]
    for head, (numerator, top, denominator) in enumerate(attend_items(items, blocks)):
        total[head_lanes(head), :] = numerator
        stat[head : head + 1, :] = top
        stat[HEADS + head : HEADS + head + 1, :] = denominator


def attend(queries, blocks, state):
    count = queries.shape[0]
    return pl.pallas_call(
        functools.partial(attend_kernel, len(blocks), state is None),
        out_shape=[
            jax.ShapeDtypeStruct((GROUP, count), F32),
            jax.ShapeDtypeStruct((8, count), F32),
        ],
        compiler_params=params(),
    )(queries, *blocks, *(() if state is None else state))


def pack_levels(levels):
    rows = []
    for level in levels:
        for _ in range(3):
            coarse = level.astype(BF16).astype(F32)
            rows.append(coarse)
            level = level - coarse
    rows.append(jnp.zeros((STATS - len(rows),) + levels[0].shape[1:], F32))
    return jnp.concatenate(rows, axis=0).astype(BF16)


def finish_kernel(start, count, *refs):
    queries, blocks, refs = refs[0], refs[1 : 1 + count], refs[1 + count :]
    old_total, old_stat, out = refs
    at = slice(start, start + 2 * TOKENS)
    items = []
    for head in range(HEADS):
        lanes = head_lanes(head)
        old = (
            old_total[lanes, at],
            old_stat[head : head + 1, at],
            old_stat[HEADS + head : HEADS + head + 1, at],
        )
        items.append((queries[at, lanes], lanes, old))
    levels = []
    for head, (numerator, top, denominator) in enumerate(attend_items(items, blocks)):
        out[head_lanes(head), :] = (numerator / denominator).astype(BF16)
        levels.append(top * SCALE2 + jnp.log2(denominator))
    out[GROUP:, :] = pack_levels(levels)


def finish(queries, blocks, state, start):
    return pl.pallas_call(
        functools.partial(finish_kernel, start, len(blocks)),
        out_shape=jax.ShapeDtypeStruct((GROUP + STATS, 2 * TOKENS), BF16),
        compiler_params=params(),
    )(queries, *blocks, *state)


def merged(parts):
    tails = [part[GROUP:].astype(F32) for part in parts]
    outs, levels = [], []
    for head in range(HEADS):
        lanes = head_lanes(head)
        first = 3 * head
        level = [
            tail[first : first + 1] + tail[first + 1 : first + 2] + tail[first + 2 : first + 3]
            for tail in tails
        ]
        top = functools.reduce(jnp.maximum, level)
        shares = [jnp.exp2(one - top) for one in level]
        whole_share = functools.reduce(jnp.add, shares)
        mixed = functools.reduce(
            jnp.add, [part[lanes].astype(F32) * share for part, share in zip(parts, shares)]
        )
        outs.append((mixed / whole_share).astype(BF16))
        levels.append(top + jnp.log2(whole_share))
    return outs, levels


def merge_kernel(mine, theirs, *outs):
    heads, levels = merged([mine[...], theirs[...]])
    packed = pack_levels(levels)
    for index, out in enumerate(outs):
        lanes = slice(index * MINE, (index + 1) * MINE)
        for head in range(HEADS):
            out[head_lanes(head), :] = heads[head][:, lanes]
        out[GROUP:, :] = packed[:, lanes]


def merge(mine, theirs):
    return pl.pallas_call(
        merge_kernel,
        out_shape=[jax.ShapeDtypeStruct((GROUP + STATS, MINE), BF16)] * 4,
        compiler_params=params(),
    )(mine, theirs)


def out_kernel(mine, across, beside, beyond, weight, other_weight, keep, *sends):
    over = (((0,), (0,)), ((), ()))
    own = jnp.concatenate(merged([mine[...], across[...]])[0], axis=0)
    other = jnp.concatenate(merged([beside[...], beyond[...]])[0], axis=0)
    for start in range(0, WIDTH, HALF):
        lanes = slice(start, start + HALF)
        product = lax.dot_general(own, weight[:, lanes], over, preferred_element_type=F32)
        product += lax.dot_general(other, other_weight[:, lanes], over, preferred_element_type=F32)
        keep[:, lanes] = product[:LOCAL]
        for index, out in enumerate(sends):
            out[:, lanes] = product[(index + 1) * LOCAL : (index + 2) * LOCAL].astype(BF16)


def out_project(parts, weight, other_weight):
    return pl.pallas_call(
        out_kernel,
        out_shape=[jax.ShapeDtypeStruct((LOCAL, WIDTH), F32)]
        + [jax.ShapeDtypeStruct((LOCAL, WIDTH), BF16)] * 3,
        compiler_params=params(),
    )(*parts, weight, other_weight)


def final_kernel(
    tokens, keep, a, b, c, gate, shift, scale, weight, bias, block_out, latent
):
    wide = lambda ref: ref[...].astype(F32)
    projected = (keep[...] + wide(a)) + (wide(b) + wide(c))
    result = (wide(tokens) + gate[...] * projected).astype(BF16)
    block_out[...] = result
    final_in = (normed(result.astype(F32)) * (1.0 + scale[...]) + shift[...]).astype(BF16)
    mixed = jnp.dot(final_in, weight[...], preferred_element_type=F32)
    latent[...] = (mixed + bias[...]).astype(BF16)


def final(tokens, parts, gate, shift, scale, weight, bias):
    return pl.pallas_call(
        final_kernel,
        out_shape=[
            jax.ShapeDtypeStruct((LOCAL, WIDTH), BF16),
            jax.ShapeDtypeStruct((LOCAL, bias.shape[1]), BF16),
        ],
        compiler_params=params(),
    )(tokens, *parts, gate, shift, scale, weight, bias)


def halo(axis, first, end):
    place = lax.axis_index(axis)
    count = lax.axis_size(axis)
    odd = place % 2 == 1
    inner = lax.ppermute(jnp.where(odd, first, end), axis, [(i, i ^ 1) for i in range(count)])
    links = [(i, i + 1) for i in range(1, count - 1, 2)]
    outer = lax.ppermute(
        jnp.where(odd, end, first), axis, links + [(target, source) for source, target in links]
    )
    inner, outer = lax.optimization_barrier((inner, outer))
    low = jnp.where(place == 0, first, jnp.where(odd, inner, outer))
    high = jnp.where(place == count - 1, end, jnp.where(odd, outer, inner))
    return low, high


def local(
    block_in,
    mod_shift,
    mod_scale,
    mod_gate,
    qkv_weight,
    q_gain,
    k_gain,
    out_weight,
    final_shift,
    final_scale,
    final_weight,
    final_bias,
    conv_weight,
    conv_bias,
):
    frames, rows, columns, width = block_in.shape
    tokens = block_in.reshape(LOCAL, WIDTH)
    core = lax.axis_index("blk") % 2
    row = lambda vector: vector.reshape(1, -1)
    left, right = modulate(tokens, mod_scale, mod_shift)
    across_left = send_uly(left, ey=1)
    rights = [right] + spread_x(right)
    pair = jnp.concatenate([left, across_left], axis=0)
    quad = jnp.concatenate(rights, axis=0)
    lefts = [pair] + spread_x(pair)
    query_weight, key_value_weight = fetch(qkv_weight, across_left)
    pieces = lefts + [quad, send_uly(quad, ey=1)]
    cosine, sine = rope_tables()

    key_value, gathered = project_key_value(pieces, key_value_weight, row(k_gain), cosine, sine)
    half = lax.dynamic_slice_in_dim(out_weight, core * (GROUP // 2), GROUP // 2, 0)
    near_chain, half = lax.optimization_barrier((key_value, half))
    far_chain = send_blk(near_chain, dc=1)
    half = send_uly(half, ex=1)
    blocks = [send_ring(near_chain), send_ring(far_chain)]
    gathered, _ = lax.optimization_barrier((gathered, far_chain))
    query = project_query(gathered, query_weight, row(q_gain), cosine, sine)
    near = jnp.concatenate([query, send_blk(query, dy=1)], axis=0)
    queries = jnp.concatenate([near, send_blk(near, dc=1)], axis=0)

    state = attend(queries, [key_value] + blocks, None)
    blocks = [send_ring(block) for block in blocks]
    later, state = lax.optimization_barrier((blocks[1], state))
    state = attend(queries, [blocks[0], later], state)
    blocks = [send_ring(blocks[0]), send_ring(later)]
    last, state = lax.optimization_barrier((blocks[0], state))
    state = attend(queries, [last, blocks[1]], state)
    last = send_ring(last)

    theirs = finish(queries, [last], state, 2 * TOKENS)
    half, theirs = lax.optimization_barrier((half, theirs))
    mine = finish(queries, [last], state, 0)
    mine, beside, across, beyond = merge(mine, send_blk(theirs, dc=1))
    half, beside = lax.optimization_barrier((half, beside))
    other_half = send_blk(half, dc=1)
    other_weight = jnp.where(
        core == 0,
        jnp.concatenate([half, other_half], axis=0),
        jnp.concatenate([other_half, half], axis=0),
    )
    beyond = send_both(beyond, 1, 1)
    parts = [mine, send_blk(across, dy=1), send_uly(beside, ex=1), beyond]
    shares = out_project(parts, out_weight, other_weight)
    parts = [
        shares[0],
        send_uly(shares[3], ex=3, ey=1),
        send_uly(shares[2], ex=3),
        send_uly(shares[1], ey=1),
    ]
    block_out, latent_tok = final(
        tokens,
        parts,
        row(mod_gate),
        row(final_shift),
        row(final_scale),
        final_weight,
        row(final_bias),
    )

    channels = final_bias.shape[0] // 4
    latent = (
        latent_tok.reshape(frames, rows, columns, channels, 2, 2)
        .transpose(0, 1, 4, 2, 5, 3)
        .reshape(frames, 2 * rows, 2 * columns, channels)
    )
    low, high = halo("blk", latent[:, :1], latent[:, -1:])
    padded = jnp.concatenate([low, latent, high], axis=1)
    low, high = halo("uly", padded[:, :, :1], padded[:, :, -1:])
    padded = jnp.concatenate([low, padded, high], axis=2)
    padded = jnp.concatenate([padded[:1], padded[:1], padded], axis=0)
    windows = []
    for time_lag in range(3):
        for row_lag in range(3):
            for column_lag in range(3):
                windows.append(
                    padded[
                        time_lag : time_lag + frames,
                        row_lag : row_lag + 2 * rows,
                        column_lag : column_lag + 2 * columns,
                    ]
                )
    patches = jnp.concatenate(windows, axis=-1)
    kernel = conv_weight.reshape(27 * channels, conv_weight.shape[-1])
    conv_out = (jnp.dot(patches, kernel, preferred_element_type=F32) + conv_bias).astype(BF16)
    return (block_out.reshape(frames, rows, columns, width), conv_out)


def solution(mesh):
    in_specs = (
        P(None, "blk", "uly", None),
        P(),
        P(),
        P(),
        P(None, None, "uly"),
        P(),
        P(),
        P("uly", None),
        P(),
        P(),
        P(),
        P(),
        P(),
        P(),
    )
    out_specs = (P(None, "blk", "uly", None), P(None, "blk", "uly", None))
    return jax.shard_map(local, mesh=mesh, in_specs=in_specs, out_specs=out_specs, check_vma=False)
```

profile of v0, /device:TPU:24, one launch (start us, length us, event | category | flops | bytes accessed | tf_op | source)
XLA Modules:
  0.0 110.6 jit_solution(16715753050012692634)
XLA Ops:
  2.7 2.8 %collective-permute-start.4 = (bf16[32,1792]{1,0:T(8,128)(2,1)S(1)}, bf16[32,1792]{1,0:T(8,128)(2,1)S(1)}, u32[]{:S(2)}, u32[]{:S(2)}) collective-permute-start(bf16[32,1792]{1,0:T(8,128)(2,1)S(1)} %get-tuple-element.42), channel_id=1, source_target_pairs={{0,6},{1,7},{2,4},{3,5},{4,2},{5,3},{6,0},{7,1},{8,14},{9,15},{10,... | collective-permute-start | bytes 344072 | tf_op jit(solution)/shard_map/ppermute | solution.py:76
  5.8 1.7 %collective-permute-start.6 = (bf16[32,1792]{1,0:T(8,128)(2,1)S(1)}, bf16[32,1792]{1,0:T(8,128)(2,1)S(1)}, u32[]{:S(2)}, u32[]{:S(2)}) collective-permute-start(bf16[32,1792]{1,0:T(8,128)(2,1)S(1)} %get-tuple-element.42), channel_id=1, source_target_pairs={{0,4},{1,5},{2,6},{3,7},{4,0},{5,1},{6,2},{7,3},{8,12},{9,13},{10,... | collective-permute-start | bytes 344072 | tf_op jit(solution)/shard_map/ppermute | solution.py:76
  9.7 1.7 %collective-permute-done.5 = bf16[32,1792]{1,0:T(8,128)(2,1)S(1)} collective-permute-done((bf16[32,1792]{1,0:T(8,128)(2,1)S(1)}, bf16[32,1792]{1,0:T(8,128)(2,1)S(1)}, u32[]{:S(2)}, u32[]{:S(2)}) %collective-permute-start.5) | collective-permute-done | bytes 114720 | tf_op jit(solution)/shard_map/ppermute | solution.py:76
  13.6 2.7 %collective-permute-start.1 = (bf16[64,1280]{1,0:T(8,128)(2,1)S(1)}, bf16[64,1280]{1,0:T(8,128)(2,1)S(1)}, u32[]{:S(2)}, u32[]{:S(2)}) collective-permute-start(bf16[64,1280]{1,0:T(8,128)(2,1)S(1)} %constant_dynamic-update-slice_fusion.a0), channel_id=1, source_target_pairs={{0,6},{1,7},{2,4},{3,5},{4,2},{5,3},{6,0},{7,1},{8,14},{9,15},{10,... | collective-permute-start | bytes 491528 | tf_op jit(solution)/shard_map/ppermute | solution.py:76
  16.2 2.1 %collective-permute-start.3 = (bf16[64,1280]{1,0:T(8,128)(2,1)S(1)}, bf16[64,1280]{1,0:T(8,128)(2,1)S(1)}, u32[]{:S(2)}, u32[]{:S(2)}) collective-permute-start(bf16[64,1280]{1,0:T(8,128)(2,1)S(1)} %constant_dynamic-update-slice_fusion.a0), channel_id=1, source_target_pairs={{0,4},{1,5},{2,6},{3,7},{4,0},{5,1},{6,2},{7,3},{8,12},{9,13},{10,... | collective-permute-start | bytes 491528 | tf_op jit(solution)/shard_map/ppermute | solution.py:76
  19.0 3.0 %copy-done.1 = bf16[3,3072,384]{2,1,0:T(8,128)(2,1)S(1)} copy-done((bf16[3,3072,384]{2,1,0:T(8,128)(2,1)S(1)}, bf16[3,3072,384]{2,1,0:T(8,128)(2,1)}, u32[]{:S(2)}) %copy-start.1) | copy-done | bytes 7077912
  22.5 1.9 %collective-permute-done.3.a3 = bf16[64,1280]{1,0:T(8,128)(2,1)S(1)} collective-permute-done((bf16[64,1280]{1,0:T(8,128)(2,1)S(1)}, bf16[64,1280]{1,0:T(8,128)(2,1)S(1)}, u32[]{:S(2)}, u32[]{:S(2)}) %collective-permute-start.3) | collective-permute-done | bytes 163872 | tf_op jit(solution)/shard_map/ppermute | solution.py:76
  24.5 1.8 %shard_map.196 = (bf16[2,256,384]{2,1,0:T(8,128)(2,1)S(1)}, bf16[256,3072]{1,0:T(8,128)(2,1)S(1)}) custom-call(bf16[64,1280]{1,0:T(8,128)(2,1)S(1)} %constant_dynamic-update-slice_fusion.a0, bf16[64,1280]{1,0:T(8,128)(2,1)S(1)} %collective-permute-done.1.a1, bf16[64,1280]{1,0:T(8,128)(2,1)S(1)} %collective-permute-done.2.a2, ...), custom_call_target="tpu_custom_call" | custom-call | tf_op jit(solution)/shard_map/pallas_call | solution.py:206
  26.4 2.0 %collective-permute-start.11 = (bf16[2,256,384]{2,1,0:T(8,128)(2,1)S(1)}, bf16[2,256,384]{2,1,0:T(8,128)(2,1)S(1)}, u32[]{:S(2)}, u32[]{:S(2)}) collective-permute-start(bf16[2,256,384]{2,1,0:T(8,128)(2,1)S(1)} %get-tuple-element.46.refs_1_), channel_id=1, source_target_pairs={{0,16},{8,120},{16,32},{24,8},{32,48},{40,24},{48,64},{56,40},{64,... | collective-permute-start | bytes 1179656 | tf_op jit(solution)/shard_map/ppermute | solution.py:72
  28.4 1.5 %shard_map.197 = bf16[256,384]{1,0:T(8,128)(2,1)S(1)} custom-call(bf16[256,3072]{1,0:T(8,128)(2,1)S(1)} %get-tuple-element.47.gathered, bf16[3072,384]{1,0:T(8,128)(2,1)S(1)} %get-tuple-element.48.weight, f32[1,128]{1,0:T(1,128)S(1)} %bitcast.27, f32[256,128]{1,0:T(8,128)S(1)} %get-tuple-element.118.cosine, f32[256,128]{1,0:T(8,128)S(1)} %get-tuple-element.117.sine), custom_call_target="tpu_custom_call" | custom-call | tf_op jit(solution)/shard_map/pallas_call | solution.py:222
  31.0 1.9 %collective-permute-start.14 = (bf16[2,256,384]{2,1,0:T(8,128)(2,1)S(1)}, bf16[2,256,384]{2,1,0:T(8,128)(2,1)S(1)}, u32[]{:S(2)}, u32[]{:S(2)}) collective-permute-start(bf16[2,256,384]{2,1,0:T(8,128)(2,1)S(1)} %collective-permute-done.8), channel_id=1, source_target_pairs={{0,16},{8,120},{16,32},{24,8},{32,48},{40,24},{48,64},{56,40},{64,... | collective-permute-start | bytes 1179656 | tf_op jit(solution)/shard_map/ppermute | solution.py:72
  33.0 5.1 %collective-permute-done.11.refs_2_ = bf16[2,256,384]{2,1,0:T(8,128)(2,1)S(1)} collective-permute-done((bf16[2,256,384]{2,1,0:T(8,128)(2,1)S(1)}, bf16[2,256,384]{2,1,0:T(8,128)(2,1)S(1)}, u32[]{:S(2)}, u32[]{:S(2)}) %collective-permute-start.11) | collective-permute-done | bytes 393248 | tf_op jit(solution)/shard_map/ppermute | solution.py:72
  38.8 2.3 %collective-permute-start.10 = (bf16[512,384]{1,0:T(8,128)(2,1)S(1)}, bf16[512,384]{1,0:T(8,128)(2,1)S(1)}, u32[]{:S(2)}, u32[]{:S(2)}) collective-permute-start(bf16[512,384]{1,0:T(8,128)(2,1)S(1)} %pad_maximum_fusion.1), channel_id=1, source_target_pairs={{0,8},{8,0},{16,24},{24,16},{32,40},{40,32},{48,56},{56,48},{64,72... | collective-permute-start | bytes 1179656 | tf_op jit(solution)/shard_map/ppermute | solution.py:68
  42.4 4.7 %collective-permute-done.12.refs_1_ = bf16[2,256,384]{2,1,0:T(8,128)(2,1)S(1)} collective-permute-done((bf16[2,256,384]{2,1,0:T(8,128)(2,1)S(1)}, bf16[2,256,384]{2,1,0:T(8,128)(2,1)S(1)}, u32[]{:S(2)}, u32[]{:S(2)}) %collective-permute-start.12) | collective-permute-done | bytes 393248 | tf_op jit(solution)/shard_map/ppermute | solution.py:72
  47.1 3.6 %shard_map.198 = (f32[384,1024]{1,0:T(8,128)S(1)}, f32[8,1024]{1,0:T(8,128)S(1)}) custom-call(bf16[1024,384]{1,0:T(8,128)(2,1)S(1)} %pad_maximum_fusion.refs_0_, bf16[2,256,384]{2,1,0:T(8,128)(2,1)S(1)} %get-tuple-element.46.refs_1_, bf16[2,256,384]{2,1,0:T(8,128)(2,1)S(1)} %collective-permute-done.11.refs_2_, ...), custom_call_target="tpu_custom_call" | custom-call | tf_op jit(solution)/shard_map/pallas_call | solution.py:308
  51.4 2.5 %shard_map.199 = (f32[384,1024]{1,0:T(8,128)S(1)}, f32[8,1024]{1,0:T(8,128)S(1)}) custom-call(bf16[1024,384]{1,0:T(8,128)(2,1)S(1)} %pad_maximum_fusion.refs_0_, bf16[2,256,384]{2,1,0:T(8,128)(2,1)S(1)} %collective-permute-done.12.refs_1_, bf16[2,256,384]{2,1,0:T(8,128)(2,1)S(1)} %collective-permute-done.15.refs_2_, ...), custom_call_target="tpu_custom_call" | custom-call | tf_op jit(solution)/shard_map/pallas_call | solution.py:308
  53.9 2.1 %collective-permute-done.13.refs_1_ = bf16[2,256,384]{2,1,0:T(8,128)(2,1)S(1)} collective-permute-done((bf16[2,256,384]{2,1,0:T(8,128)(2,1)S(1)}, bf16[2,256,384]{2,1,0:T(8,128)(2,1)S(1)}, u32[]{:S(2)}, u32[]{:S(2)}) %collective-permute-start.13) | collective-permute-done | bytes 393248 | tf_op jit(solution)/shard_map/ppermute | solution.py:72
  56.6 3.7 %collective-permute-done.17.refs_2_ = bf16[2,256,384]{2,1,0:T(8,128)(2,1)S(1)} collective-permute-done((bf16[2,256,384]{2,1,0:T(8,128)(2,1)S(1)}, bf16[2,256,384]{2,1,0:T(8,128)(2,1)S(1)}, u32[]{:S(2)}, u32[]{:S(2)}) %collective-permute-start.17) | collective-permute-done | bytes 393248 | tf_op jit(solution)/shard_map/ppermute | solution.py:72
  60.3 2.5 %shard_map.200 = (f32[384,1024]{1,0:T(8,128)S(1)}, f32[8,1024]{1,0:T(8,128)S(1)}) custom-call(bf16[1024,384]{1,0:T(8,128)(2,1)S(1)} %pad_maximum_fusion.refs_0_, bf16[2,256,384]{2,1,0:T(8,128)(2,1)S(1)} %collective-permute-done.13.refs_1_, bf16[2,256,384]{2,1,0:T(8,128)(2,1)S(1)} %collective-permute-done.17.refs_2_, ...), custom_call_target="tpu_custom_call" | custom-call | tf_op jit(solution)/shard_map/pallas_call | solution.py:308
  62.9 2.1 %collective-permute-done.16.refs_1_ = bf16[2,256,384]{2,1,0:T(8,128)(2,1)S(1)} collective-permute-done((bf16[2,256,384]{2,1,0:T(8,128)(2,1)S(1)}, bf16[2,256,384]{2,1,0:T(8,128)(2,1)S(1)}, u32[]{:S(2)}, u32[]{:S(2)}) %collective-permute-start.16) | collective-permute-done | bytes 393248 | tf_op jit(solution)/shard_map/ppermute | solution.py:72
  69.5 1.4 %collective-permute-start.20 = (bf16[400,128]{1,0:T(8,128)(2,1)S(1)}, bf16[400,128]{1,0:T(8,128)(2,1)S(1)}, u32[]{:S(2)}, u32[]{:S(2)}) collective-permute-start(bf16[400,128]{1,0:T(8,128)(2,1)S(1)} %get-tuple-element.64), channel_id=1, source_target_pairs={{0,128},{8,136},{16,144},{24,152},{32,160},{40,168},{48,176},{56,1... | collective-permute-start | bytes 307208 | tf_op jit(solution)/shard_map/ppermute | solution.py:68
  70.9 2.9 %collective-permute-start.22 = (bf16[400,128]{1,0:T(8,128)(2,1)S(1)}, bf16[400,128]{1,0:T(8,128)(2,1)S(1)}, u32[]{:S(2)}, u32[]{:S(2)}) collective-permute-start(bf16[400,128]{1,0:T(8,128)(2,1)S(1)} %get-tuple-element.68), channel_id=1, source_target_pairs={{0,130},{1,131},{2,128},{3,129},{4,134},{5,135},{6,132},{7,133},{8... | collective-permute-start | bytes 307208 | tf_op jit(solution)/shard_map/ppermute | solution.py:91
  75.7 2.3 %collective-permute-done.22.beyond = bf16[400,128]{1,0:T(8,128)(2,1)S(1)} collective-permute-done((bf16[400,128]{1,0:T(8,128)(2,1)S(1)}, bf16[400,128]{1,0:T(8,128)(2,1)S(1)}, u32[]{:S(2)}, u32[]{:S(2)}) %collective-permute-start.22) | collective-permute-done | bytes 102432 | tf_op jit(solution)/shard_map/ppermute | solution.py:91
  79.1 2.3 %collective-permute-start.24 = (bf16[32,3072]{1,0:T(8,128)(2,1)S(1)}, bf16[32,3072]{1,0:T(8,128)(2,1)S(1)}, u32[]{:S(2)}, u32[]{:S(2)}) collective-permute-start(bf16[32,3072]{1,0:T(8,128)(2,1)S(1)} %get-tuple-element.71), channel_id=1, source_target_pairs={{0,7},{1,6},{2,5},{3,4},{4,3},{5,2},{6,1},{7,0},{8,15},{9,14},{10,... | collective-permute-start | bytes 589832 | tf_op jit(solution)/shard_map/ppermute | solution.py:76
  81.3 1.8 %collective-permute-start.25 = (bf16[32,3072]{1,0:T(8,128)(2,1)S(1)}, bf16[32,3072]{1,0:T(8,128)(2,1)S(1)}, u32[]{:S(2)}, u32[]{:S(2)}) collective-permute-start(bf16[32,3072]{1,0:T(8,128)(2,1)S(1)} %get-tuple-element.72), channel_id=1, source_target_pairs={{0,6},{1,7},{2,4},{3,5},{4,2},{5,3},{6,0},{7,1},{8,14},{9,15},{10,... | collective-permute-start | bytes 589832 | tf_op jit(solution)/shard_map/ppermute | solution.py:76
  84.2 4.6 %collective-permute-done.24.a = bf16[32,3072]{1,0:T(8,128)(2,1)S(1)} collective-permute-done((bf16[32,3072]{1,0:T(8,128)(2,1)S(1)}, bf16[32,3072]{1,0:T(8,128)(2,1)S(1)}, u32[]{:S(2)}, u32[]{:S(2)}) %collective-permute-start.24) | collective-permute-done | bytes 196640 | tf_op jit(solution)/shard_map/ppermute | solution.py:76
  88.8 1.9 %collective-permute-done.25.b = bf16[32,3072]{1,0:T(8,128)(2,1)S(1)} collective-permute-done((bf16[32,3072]{1,0:T(8,128)(2,1)S(1)}, bf16[32,3072]{1,0:T(8,128)(2,1)S(1)}, u32[]{:S(2)}, u32[]{:S(2)}) %collective-permute-start.25) | collective-permute-done | bytes 196640 | tf_op jit(solution)/shard_map/ppermute | solution.py:76
  92.6 5.9 %collective-permute-start.28 = (bf16[2,1,16,16]{3,2,1,0:T(8,128)(2,1)S(1)}, bf16[2,1,16,16]{3,2,1,0:T(8,128)(2,1)S(1)}, u32[]{:S(2)}, u32[]{:S(2)}) collective-permute-start(bf16[2,1,16,16]{3,2,1,0:T(8,128)(2,1)S(1)} %get-tuple-element.113), channel_id=1, source_target_pairs={{8,16},{24,32},{40,48},{56,64},{72,80},{88,96},{104,112},{120,128}... | collective-permute-start | bytes 3080 | tf_op jit(solution)/shard_map/ppermute | solution.py:447
  98.5 2.7 %collective-permute-done.28 = bf16[2,1,16,16]{3,2,1,0:T(8,128)(2,1)S(1)} collective-permute-done((bf16[2,1,16,16]{3,2,1,0:T(8,128)(2,1)S(1)}, bf16[2,1,16,16]{3,2,1,0:T(8,128)(2,1)S(1)}, u32[]{:S(2)}, u32[]{:S(2)}) %collective-permute-start.28) | collective-permute-done | bytes 1056 | tf_op jit(solution)/shard_map/ppermute | solution.py:447
  101.2 1.4 %collective-permute-start.29 = (bf16[2,6,1,16]{3,2,1,0:T(2,128)(2,1)S(1)}, bf16[2,6,1,16]{3,2,1,0:T(2,128)(2,1)S(1)}, u32[]{:S(2)}, u32[]{:S(2)}) collective-permute-start(bf16[2,6,1,16]{3,2,1,0:T(2,128)(2,1)S(1)} %broadcast_select_fusion.4), channel_id=1, source_target_pairs={{0,1},{1,0},{2,3},{3,2},{4,5},{5,4},{6,7},{7,6},{8,9},{9,8},{10,11... | collective-permute-start | bytes 1160 | tf_op jit(solution)/shard_map/ppermute | solution.py:445
  102.6 2.2 %collective-permute-start.30 = (bf16[2,6,1,16]{3,2,1,0:T(2,128)(2,1)S(1)}, bf16[2,6,1,16]{3,2,1,0:T(2,128)(2,1)S(1)}, u32[]{:S(2)}, u32[]{:S(2)}) collective-permute-start(bf16[2,6,1,16]{3,2,1,0:T(2,128)(2,1)S(1)} %get-tuple-element.80), channel_id=1, source_target_pairs={{1,2},{3,4},{5,6},{2,1},{4,3},{6,5},{9,10},{11,12},{13,14},{10,9},... | collective-permute-start | bytes 1160 | tf_op jit(solution)/shard_map/ppermute | solution.py:447
  104.9 4.1 %collective-permute-done.30 = bf16[2,6,1,16]{3,2,1,0:T(2,128)(2,1)S(1)} collective-permute-done((bf16[2,6,1,16]{3,2,1,0:T(2,128)(2,1)S(1)}, bf16[2,6,1,16]{3,2,1,0:T(2,128)(2,1)S(1)}, u32[]{:S(2)}, u32[]{:S(2)}) %collective-permute-start.30) | collective-permute-done | bytes 416 | tf_op jit(solution)/shard_map/ppermute | solution.py:447
  (109 shorter events, 24.2 us)
Async XLA Ops:
  0.6 109.0 %copy-start = (bf16[3,3,3,16,512]{4,3,2,1,0:T(8,128)(2,1)S(1)}, bf16[3,3,3,16,512]{4,3,2,1,0:T(8,128)(2,1)}, u32[]{:S(2)}) copy-start(bf16[3,3,3,16,512]{4,3,2,1,0:T(8,128)(2,1)} %param.31) | copy-start | bytes 1327108
  2.7 7.0 %collective-permute-start.4 = (bf16[32,1792]{1,0:T(8,128)(2,1)S(1)}, bf16[32,1792]{1,0:T(8,128)(2,1)S(1)}, u32[]{:S(2)}, u32[]{:S(2)}) collective-permute-start(bf16[32,1792]{1,0:T(8,128)(2,1)S(1)} %get-tuple-element.42), channel_id=1, source_target_pairs={{0,6},{1,7},{2,4},{3,5},{4,2},{5,3},{6,0},{7,1},{8,14},{9,15},{10,... | collective-permute-start | bytes 344072 | tf_op jit(solution)/shard_map/ppermute | solution.py:76
  5.6 5.8 %collective-permute-start.5 = (bf16[32,1792]{1,0:T(8,128)(2,1)S(1)}, bf16[32,1792]{1,0:T(8,128)(2,1)S(1)}, u32[]{:S(2)}, u32[]{:S(2)}) collective-permute-start(bf16[32,1792]{1,0:T(8,128)(2,1)S(1)} %get-tuple-element.42), channel_id=1, source_target_pairs={{0,2},{1,3},{2,0},{3,1},{4,6},{5,7},{6,4},{7,5},{8,10},{9,11},{10,... | collective-permute-start | bytes 344072 | tf_op jit(solution)/shard_map/ppermute | solution.py:76
  5.8 6.9 %collective-permute-start.6 = (bf16[32,1792]{1,0:T(8,128)(2,1)S(1)}, bf16[32,1792]{1,0:T(8,128)(2,1)S(1)}, u32[]{:S(2)}, u32[]{:S(2)}) collective-permute-start(bf16[32,1792]{1,0:T(8,128)(2,1)S(1)} %get-tuple-element.42), channel_id=1, source_target_pairs={{0,4},{1,5},{2,6},{3,7},{4,0},{5,1},{6,2},{7,3},{8,12},{9,13},{10,... | collective-permute-start | bytes 344072 | tf_op jit(solution)/shard_map/ppermute | solution.py:76
  7.5 6.1 %collective-permute-start = (bf16[32,1280]{1,0:T(8,128)(2,1)S(1)}, bf16[32,1280]{1,0:T(8,128)(2,1)S(1)}, u32[]{:S(2)}, u32[]{:S(2)}) collective-permute-start(bf16[32,1280]{1,0:T(8,128)(2,1)S(1)} %get-tuple-element.41), channel_id=1, source_target_pairs={{0,1},{1,0},{2,3},{3,2},{4,5},{5,4},{6,7},{7,6},{8,9},{9,8},{10,11... | collective-permute-start | bytes 245768 | tf_op jit(solution)/shard_map/ppermute | solution.py:76
  12.7 11.7 %collective-permute-start.7 = (bf16[128,1792]{1,0:T(8,128)(2,1)S(1)}, bf16[128,1792]{1,0:T(8,128)(2,1)S(1)}, u32[]{:S(2)}, u32[]{:S(2)}) collective-permute-start(bf16[128,1792]{1,0:T(8,128)(2,1)S(1)} %constant_dynamic-update-slice_fusion.2.b0), channel_id=1, source_target_pairs={{0,1},{1,0},{2,3},{3,2},{4,5},{5,4},{6,7},{7,6},{8,9},{9,8},{10,11... | collective-permute-start | bytes 1376264 | tf_op jit(solution)/shard_map/ppermute | solution.py:76
  13.6 8.9 %collective-permute-start.1 = (bf16[64,1280]{1,0:T(8,128)(2,1)S(1)}, bf16[64,1280]{1,0:T(8,128)(2,1)S(1)}, u32[]{:S(2)}, u32[]{:S(2)}) collective-permute-start(bf16[64,1280]{1,0:T(8,128)(2,1)S(1)} %constant_dynamic-update-slice_fusion.a0), channel_id=1, source_target_pairs={{0,6},{1,7},{2,4},{3,5},{4,2},{5,3},{6,0},{7,1},{8,14},{9,15},{10,... | collective-permute-start | bytes 491528 | tf_op jit(solution)/shard_map/ppermute | solution.py:76
  16.2 6.3 %collective-permute-start.2 = (bf16[64,1280]{1,0:T(8,128)(2,1)S(1)}, bf16[64,1280]{1,0:T(8,128)(2,1)S(1)}, u32[]{:S(2)}, u32[]{:S(2)}) collective-permute-start(bf16[64,1280]{1,0:T(8,128)(2,1)S(1)} %constant_dynamic-update-slice_fusion.a0), channel_id=1, source_target_pairs={{0,2},{1,3},{2,0},{3,1},{4,6},{5,7},{6,4},{7,5},{8,10},{9,11},{10,... | collective-permute-start | bytes 491528 | tf_op jit(solution)/shard_map/ppermute | solution.py:76
  16.2 8.2 %collective-permute-start.3 = (bf16[64,1280]{1,0:T(8,128)(2,1)S(1)}, bf16[64,1280]{1,0:T(8,128)(2,1)S(1)}, u32[]{:S(2)}, u32[]{:S(2)}) collective-permute-start(bf16[64,1280]{1,0:T(8,128)(2,1)S(1)} %constant_dynamic-update-slice_fusion.a0), channel_id=1, source_target_pairs={{0,4},{1,5},{2,6},{3,7},{4,0},{5,1},{6,2},{7,3},{8,12},{9,13},{10,... | collective-permute-start | bytes 491528 | tf_op jit(solution)/shard_map/ppermute | solution.py:76
  26.3 2.1 %collective-permute-start.8 = (bf16[2,256,384]{2,1,0:T(8,128)(2,1)S(1)}, bf16[2,256,384]{2,1,0:T(8,128)(2,1)S(1)}, u32[]{:S(2)}, u32[]{:S(2)}) collective-permute-start(bf16[2,256,384]{2,1,0:T(8,128)(2,1)S(1)} %get-tuple-element.46.refs_1_), channel_id=1, source_target_pairs={{0,8},{8,0},{16,24},{24,16},{32,40},{40,32},{48,56},{56,48},{64,72... | collective-permute-start | bytes 1179656 | tf_op jit(solution)/shard_map/ppermute | solution.py:68
  26.4 11.7 %collective-permute-start.11 = (bf16[2,256,384]{2,1,0:T(8,128)(2,1)S(1)}, bf16[2,256,384]{2,1,0:T(8,128)(2,1)S(1)}, u32[]{:S(2)}, u32[]{:S(2)}) collective-permute-start(bf16[2,256,384]{2,1,0:T(8,128)(2,1)S(1)} %get-tuple-element.46.refs_1_), channel_id=1, source_target_pairs={{0,16},{8,120},{16,32},{24,8},{32,48},{40,24},{48,64},{56,40},{64,... | collective-permute-start | bytes 1179656 | tf_op jit(solution)/shard_map/ppermute | solution.py:72
  29.9 8.9 %collective-permute-start.9 = (bf16[256,384]{1,0:T(8,128)(2,1)S(1)}, bf16[256,384]{1,0:T(8,128)(2,1)S(1)}, u32[]{:S(2)}, u32[]{:S(2)}) collective-permute-start(bf16[256,384]{1,0:T(8,128)(2,1)S(1)} %shard_map.197), channel_id=1, source_target_pairs={{0,128},{8,136},{16,144},{24,152},{32,160},{40,168},{48,176},{56,1... | collective-permute-start | bytes 589832 | tf_op jit(solution)/shard_map/ppermute | solution.py:68
  31.0 11.3 %collective-permute-start.14 = (bf16[2,256,384]{2,1,0:T(8,128)(2,1)S(1)}, bf16[2,256,384]{2,1,0:T(8,128)(2,1)S(1)}, u32[]{:S(2)}, u32[]{:S(2)}) collective-permute-start(bf16[2,256,384]{2,1,0:T(8,128)(2,1)S(1)} %collective-permute-done.8), channel_id=1, source_target_pairs={{0,16},{8,120},{16,32},{24,8},{32,48},{40,24},{48,64},{56,40},{64,... | collective-permute-start | bytes 1179656 | tf_op jit(solution)/shard_map/ppermute | solution.py:72
  38.1 9.0 %collective-permute-start.12 = (bf16[2,256,384]{2,1,0:T(8,128)(2,1)S(1)}, bf16[2,256,384]{2,1,0:T(8,128)(2,1)S(1)}, u32[]{:S(2)}, u32[]{:S(2)}) collective-permute-start(bf16[2,256,384]{2,1,0:T(8,128)(2,1)S(1)} %collective-permute-done.11.refs_2_), channel_id=1, source_target_pairs={{0,16},{8,120},{16,32},{24,8},{32,48},{40,24},{48,64},{56,40},{64,... | collective-permute-start | bytes 1179656 | tf_op jit(solution)/shard_map/ppermute | solution.py:72
  38.1 27.8 %collective-permute-start.18 = (bf16[192,3072]{1,0:T(8,128)(2,1)S(1)}, bf16[192,3072]{1,0:T(8,128)(2,1)S(1)}, u32[]{:S(2)}, u32[]{:S(2)}) collective-permute-start(bf16[192,3072]{1,0:T(8,128)(2,1)S(1)} %constant_dynamic-slice_fusion), channel_id=1, source_target_pairs={{0,2},{1,3},{2,0},{3,1},{4,6},{5,7},{6,4},{7,5},{8,10},{9,11},{10,... | collective-permute-start | bytes 3538952 | tf_op jit(solution)/shard_map/ppermute | solution.py:76
  38.8 8.3 %collective-permute-start.10 = (bf16[512,384]{1,0:T(8,128)(2,1)S(1)}, bf16[512,384]{1,0:T(8,128)(2,1)S(1)}, u32[]{:S(2)}, u32[]{:S(2)}) collective-permute-start(bf16[512,384]{1,0:T(8,128)(2,1)S(1)} %pad_maximum_fusion.1), channel_id=1, source_target_pairs={{0,8},{8,0},{16,24},{24,16},{32,40},{40,32},{48,56},{56,48},{64,72... | collective-permute-start | bytes 1179656 | tf_op jit(solution)/shard_map/ppermute | solution.py:68
  42.4 9.0 %collective-permute-start.15 = (bf16[2,256,384]{2,1,0:T(8,128)(2,1)S(1)}, bf16[2,256,384]{2,1,0:T(8,128)(2,1)S(1)}, u32[]{:S(2)}, u32[]{:S(2)}) collective-permute-start(bf16[2,256,384]{2,1,0:T(8,128)(2,1)S(1)} %collective-permute-done.14.refs_3_), channel_id=1, source_target_pairs={{0,16},{8,120},{16,32},{24,8},{32,48},{40,24},{48,64},{56,40},{64,... | collective-permute-start | bytes 1179656 | tf_op jit(solution)/shard_map/ppermute | solution.py:72
  47.1 9.0 %collective-permute-start.13 = (bf16[2,256,384]{2,1,0:T(8,128)(2,1)S(1)}, bf16[2,256,384]{2,1,0:T(8,128)(2,1)S(1)}, u32[]{:S(2)}, u32[]{:S(2)}) collective-permute-start(bf16[2,256,384]{2,1,0:T(8,128)(2,1)S(1)} %collective-permute-done.12.refs_1_), channel_id=1, source_target_pairs={{0,16},{8,120},{16,32},{24,8},{32,48},{40,24},{48,64},{56,40},{64,... | collective-permute-start | bytes 1179656 | tf_op jit(solution)/shard_map/ppermute | solution.py:72
  51.3 9.0 %collective-permute-start.17 = (bf16[2,256,384]{2,1,0:T(8,128)(2,1)S(1)}, bf16[2,256,384]{2,1,0:T(8,128)(2,1)S(1)}, u32[]{:S(2)}, u32[]{:S(2)}) collective-permute-start(bf16[2,256,384]{2,1,0:T(8,128)(2,1)S(1)} %collective-permute-done.15.refs_2_), channel_id=1, source_target_pairs={{0,16},{8,120},{16,32},{24,8},{32,48},{40,24},{48,64},{56,40},{64,... | collective-permute-start | bytes 1179656 | tf_op jit(solution)/shard_map/ppermute | solution.py:72
  56.0 9.0 %collective-permute-start.16 = (bf16[2,256,384]{2,1,0:T(8,128)(2,1)S(1)}, bf16[2,256,384]{2,1,0:T(8,128)(2,1)S(1)}, u32[]{:S(2)}, u32[]{:S(2)}) collective-permute-start(bf16[2,256,384]{2,1,0:T(8,128)(2,1)S(1)} %collective-permute-done.13.refs_1_), channel_id=1, source_target_pairs={{0,16},{8,120},{16,32},{24,8},{32,48},{40,24},{48,64},{56,40},{64,... | collective-permute-start | bytes 1179656 | tf_op jit(solution)/shard_map/ppermute | solution.py:72
  65.9 2.2 %collective-permute-start.19 = (bf16[400,512]{1,0:T(8,128)(2,1)S(1)}, bf16[400,512]{1,0:T(8,128)(2,1)S(1)}, u32[]{:S(2)}, u32[]{:S(2)}) collective-permute-start(bf16[400,512]{1,0:T(8,128)(2,1)S(1)} %shard_map.202), channel_id=1, source_target_pairs={{0,8},{8,0},{16,24},{24,16},{32,40},{40,32},{48,56},{56,48},{64,72... | collective-permute-start | bytes 1228808 | tf_op jit(solution)/shard_map/ppermute | solution.py:68
  68.4 5.5 %collective-permute-start.23 = (bf16[192,3072]{1,0:T(8,128)(2,1)S(1)}, bf16[192,3072]{1,0:T(8,128)(2,1)S(1)}, u32[]{:S(2)}, u32[]{:S(2)}) collective-permute-start(bf16[192,3072]{1,0:T(8,128)(2,1)S(1)} %collective-permute-done.18), channel_id=1, source_target_pairs={{0,8},{8,0},{16,24},{24,16},{32,40},{40,32},{48,56},{56,48},{64,72... | collective-permute-start | bytes 3538952 | tf_op jit(solution)/shard_map/ppermute | solution.py:68
  68.8 5.9 %collective-permute-start.21 = (bf16[400,128]{1,0:T(8,128)(2,1)S(1)}, bf16[400,128]{1,0:T(8,128)(2,1)S(1)}, u32[]{:S(2)}, u32[]{:S(2)}) collective-permute-start(bf16[400,128]{1,0:T(8,128)(2,1)S(1)} %get-tuple-element.67), channel_id=1, source_target_pairs={{0,2},{1,3},{2,0},{3,1},{4,6},{5,7},{6,4},{7,5},{8,10},{9,11},{10,... | collective-permute-start | bytes 307208 | tf_op jit(solution)/shard_map/ppermute | solution.py:76
  69.5 6.2 %collective-permute-start.20 = (bf16[400,128]{1,0:T(8,128)(2,1)S(1)}, bf16[400,128]{1,0:T(8,128)(2,1)S(1)}, u32[]{:S(2)}, u32[]{:S(2)}) collective-permute-start(bf16[400,128]{1,0:T(8,128)(2,1)S(1)} %get-tuple-element.64), channel_id=1, source_target_pairs={{0,128},{8,136},{16,144},{24,152},{32,160},{40,168},{48,176},{56,1... | collective-permute-start | bytes 307208 | tf_op jit(solution)/shard_map/ppermute | solution.py:68
  70.9 7.1 %collective-permute-start.22 = (bf16[400,128]{1,0:T(8,128)(2,1)S(1)}, bf16[400,128]{1,0:T(8,128)(2,1)S(1)}, u32[]{:S(2)}, u32[]{:S(2)}) collective-permute-start(bf16[400,128]{1,0:T(8,128)(2,1)S(1)} %get-tuple-element.68), channel_id=1, source_target_pairs={{0,130},{1,131},{2,128},{3,129},{4,134},{5,135},{6,132},{7,133},{8... | collective-permute-start | bytes 307208 | tf_op jit(solution)/shard_map/ppermute | solution.py:91
  79.1 9.8 %collective-permute-start.24 = (bf16[32,3072]{1,0:T(8,128)(2,1)S(1)}, bf16[32,3072]{1,0:T(8,128)(2,1)S(1)}, u32[]{:S(2)}, u32[]{:S(2)}) collective-permute-start(bf16[32,3072]{1,0:T(8,128)(2,1)S(1)} %get-tuple-element.71), channel_id=1, source_target_pairs={{0,7},{1,6},{2,5},{3,4},{4,3},{5,2},{6,1},{7,0},{8,15},{9,14},{10,... | collective-permute-start | bytes 589832 | tf_op jit(solution)/shard_map/ppermute | solution.py:76
  81.3 9.4 %collective-permute-start.25 = (bf16[32,3072]{1,0:T(8,128)(2,1)S(1)}, bf16[32,3072]{1,0:T(8,128)(2,1)S(1)}, u32[]{:S(2)}, u32[]{:S(2)}) collective-permute-start(bf16[32,3072]{1,0:T(8,128)(2,1)S(1)} %get-tuple-element.72), channel_id=1, source_target_pairs={{0,6},{1,7},{2,4},{3,5},{4,2},{5,3},{6,0},{7,1},{8,14},{9,15},{10,... | collective-permute-start | bytes 589832 | tf_op jit(solution)/shard_map/ppermute | solution.py:76
  83.1 7.8 %collective-permute-start.26 = (bf16[32,3072]{1,0:T(8,128)(2,1)S(1)}, bf16[32,3072]{1,0:T(8,128)(2,1)S(1)}, u32[]{:S(2)}, u32[]{:S(2)}) collective-permute-start(bf16[32,3072]{1,0:T(8,128)(2,1)S(1)} %get-tuple-element.73), channel_id=1, source_target_pairs={{0,1},{1,0},{2,3},{3,2},{4,5},{5,4},{6,7},{7,6},{8,9},{9,8},{10,11... | collective-permute-start | bytes 589832 | tf_op jit(solution)/shard_map/ppermute | solution.py:76
  92.5 6.0 %collective-permute-start.27 = (bf16[2,1,16,16]{3,2,1,0:T(8,128)(2,1)S(1)}, bf16[2,1,16,16]{3,2,1,0:T(8,128)(2,1)S(1)}, u32[]{:S(2)}, u32[]{:S(2)}) collective-permute-start(bf16[2,1,16,16]{3,2,1,0:T(8,128)(2,1)S(1)} %get-tuple-element.114), channel_id=1, source_target_pairs={{0,8},{8,0},{16,24},{24,16},{32,40},{40,32},{48,56},{56,48},{64,72... | collective-permute-start | bytes 3080 | tf_op jit(solution)/shard_map/ppermute | solution.py:445
  92.6 8.6 %collective-permute-start.28 = (bf16[2,1,16,16]{3,2,1,0:T(8,128)(2,1)S(1)}, bf16[2,1,16,16]{3,2,1,0:T(8,128)(2,1)S(1)}, u32[]{:S(2)}, u32[]{:S(2)}) collective-permute-start(bf16[2,1,16,16]{3,2,1,0:T(8,128)(2,1)S(1)} %get-tuple-element.113), channel_id=1, source_target_pairs={{8,16},{24,32},{40,48},{56,64},{72,80},{88,96},{104,112},{120,128}... | collective-permute-start | bytes 3080 | tf_op jit(solution)/shard_map/ppermute | solution.py:447
  101.2 3.7 %collective-permute-start.29 = (bf16[2,6,1,16]{3,2,1,0:T(2,128)(2,1)S(1)}, bf16[2,6,1,16]{3,2,1,0:T(2,128)(2,1)S(1)}, u32[]{:S(2)}, u32[]{:S(2)}) collective-permute-start(bf16[2,6,1,16]{3,2,1,0:T(2,128)(2,1)S(1)} %broadcast_select_fusion.4), channel_id=1, source_target_pairs={{0,1},{1,0},{2,3},{3,2},{4,5},{5,4},{6,7},{7,6},{8,9},{9,8},{10,11... | collective-permute-start | bytes 1160 | tf_op jit(solution)/shard_map/ppermute | solution.py:445
  102.6 6.4 %collective-permute-start.30 = (bf16[2,6,1,16]{3,2,1,0:T(2,128)(2,1)S(1)}, bf16[2,6,1,16]{3,2,1,0:T(2,128)(2,1)S(1)}, u32[]{:S(2)}, u32[]{:S(2)}) collective-permute-start(bf16[2,6,1,16]{3,2,1,0:T(2,128)(2,1)S(1)} %get-tuple-element.80), channel_id=1, source_target_pairs={{1,2},{3,4},{5,6},{2,1},{4,3},{6,5},{9,10},{11,12},{13,14},{10,9},... | collective-permute-start | bytes 1160 | tf_op jit(solution)/shard_map/ppermute | solution.py:447
  (16 other events, 177.6 us)
where the time goes:
time: 111 us
  waiting for transfers between devices  41.7 us (38%)
  starting transfers between devices  40.6 us (37%)
  Pallas kernels  17 us (15%)
  local copies, waits for them, and re-layouts  6.51 us (6%)
  other arithmetic  2.75 us (2%)
  between operations  1.17 us (1%)
    ppermute x7, waiting for transfers between devices, send_ring(): return lax.ppermute(value, 'blk', ring_pairs())  19.6 us
    ppermute x13, starting transfers between devices, send_uly(): return lax.ppermute(value, 'uly', uly_pairs(ex, ey))  17.2 us
    ppermute x13, waiting for transfers between devices, send_uly(): return lax.ppermute(value, 'uly', uly_pairs(ex, ey))  11.6 us
    pallas_call x3, Pallas kernels, attend(): pl.pallas_call(functools.partial(attend_kernel, len(blocks), state is Non...  8.68 us
    ppermute x2, starting transfers between devices, halo(): lax.ppermute(jnp.where(odd, end, first), axis, links + [(target, source)...  8.12 us
    ppermute x2, waiting for transfers between devices, halo(): lax.ppermute(jnp.where(odd, end, first), axis, links + [(target, source)...  6.72 us
    ppermute x6, starting transfers between devices, send_blk(): return lax.ppermute(value, 'blk', blk_pairs(dy, dz, dc))  6.25 us
    ppermute x7, starting transfers between devices, send_ring(): return lax.ppermute(value, 'blk', ring_pairs())  4.52 us
  transfers between devices with their start and end apart: 31, of which 19 were waited for; matrix products, arithmetic and copies ran while one was open for 3% of the time, Pallas kernels for 11%

commit v1 on v0

--- a/solution.py
+++ b/solution.py
@@ -496,11 +496,11 @@
 
     state = attend(queries, [key_value] + blocks, None)
     blocks = [send_ring(block) for block in blocks]
-    later, state = lax.optimization_barrier((blocks[1], state))
-    state = attend(queries, [blocks[0], later], state)
-    blocks = [send_ring(blocks[0]), send_ring(later)]
-    last, state = lax.optimization_barrier((blocks[0], state))
-    state = attend(queries, [last, blocks[1]], state)
+    second = blocks
+    third = [send_ring(block) for block in second]
+    last, state = lax.optimization_barrier((third[0], state))
+    state = attend(queries, second, state)
+    state = attend(queries, [last, third[1]], state)
     last = send_ring(last)
 
     theirs = finish(queries, [last], state, 2 * TOKENS)

time: 111 us -> 111 us (level)
  no operation moved by 1% of the time
where the time goes in v1:
time: 111 us
  waiting for transfers between devices  42.3 us (38%)
  starting transfers between devices  40 us (36%)
  Pallas kernels  17 us (15%)
  local copies, waits for them, and re-layouts  6.51 us (6%)
  other arithmetic  2.75 us (2%)
  between operations  1.17 us (1%)
    ppermute x7, waiting for transfers between devices, send_ring(): return lax.ppermute(value, 'blk', ring_pairs())  20.2 us
    ppermute x13, starting transfers between devices, send_uly(): return lax.ppermute(value, 'uly', uly_pairs(ex, ey))  17.3 us
    ppermute x13, waiting for transfers between devices, send_uly(): return lax.ppermute(value, 'uly', uly_pairs(ex, ey))  11.6 us
    pallas_call x3, Pallas kernels, attend(): pl.pallas_call(functools.partial(attend_kernel, len(blocks), state is Non...  8.7 us
    ppermute x2, starting transfers between devices, halo(): lax.ppermute(jnp.where(odd, end, first), axis, links + [(target, source)...  8.12 us
    ppermute x2, waiting for transfers between devices, halo(): lax.ppermute(jnp.where(odd, end, first), axis, links + [(target, source)...  6.73 us
    ppermute x6, starting transfers between devices, send_blk(): return lax.ppermute(value, 'blk', blk_pairs(dy, dz, dc))  6.24 us
    unnamed x39, local copies, waits for them, and re-layouts  4.42 us
  transfers between devices with their start and end apart: 31, of which 19 were waited for; matrix products, arithmetic and copies ran while one was open for 3% of the time, Pallas kernels for 11%

profile of v1, /device:TPU:24, one launch (start us, length us, event | category | flops | bytes accessed | tf_op | source)
XLA Modules:
  0.0 110.6 jit_solution(4095179095555413231)
XLA Ops:
  2.7 2.8 %collective-permute-start.4 = (bf16[32,1792]{1,0:T(8,128)(2,1)S(1)}, bf16[32,1792]{1,0:T(8,128)(2,1)S(1)}, u32[]{:S(2)}, u32[]{:S(2)}) collective-permute-start(bf16[32,1792]{1,0:T(8,128)(2,1)S(1)} %get-tuple-element.39), channel_id=1, source_target_pairs={{0,6},{1,7},{2,4},{3,5},{4,2},{5,3},{6,0},{7,1},{8,14},{9,15},{10,... | collective-permute-start | bytes 344072 | tf_op jit(solution)/shard_map/ppermute | solution.py:76
  5.8 1.7 %collective-permute-start.6 = (bf16[32,1792]{1,0:T(8,128)(2,1)S(1)}, bf16[32,1792]{1,0:T(8,128)(2,1)S(1)}, u32[]{:S(2)}, u32[]{:S(2)}) collective-permute-start(bf16[32,1792]{1,0:T(8,128)(2,1)S(1)} %get-tuple-element.39), channel_id=1, source_target_pairs={{0,4},{1,5},{2,6},{3,7},{4,0},{5,1},{6,2},{7,3},{8,12},{9,13},{10,... | collective-permute-start | bytes 344072 | tf_op jit(solution)/shard_map/ppermute | solution.py:76
  9.7 1.7 %collective-permute-done.5 = bf16[32,1792]{1,0:T(8,128)(2,1)S(1)} collective-permute-done((bf16[32,1792]{1,0:T(8,128)(2,1)S(1)}, bf16[32,1792]{1,0:T(8,128)(2,1)S(1)}, u32[]{:S(2)}, u32[]{:S(2)}) %collective-permute-start.5) | collective-permute-done | bytes 114720 | tf_op jit(solution)/shard_map/ppermute | solution.py:76
  13.6 2.7 %collective-permute-start.1 = (bf16[64,1280]{1,0:T(8,128)(2,1)S(1)}, bf16[64,1280]{1,0:T(8,128)(2,1)S(1)}, u32[]{:S(2)}, u32[]{:S(2)}) collective-permute-start(bf16[64,1280]{1,0:T(8,128)(2,1)S(1)} %constant_dynamic-update-slice_fusion.a0), channel_id=1, source_target_pairs={{0,6},{1,7},{2,4},{3,5},{4,2},{5,3},{6,0},{7,1},{8,14},{9,15},{10,... | collective-permute-start | bytes 491528 | tf_op jit(solution)/shard_map/ppermute | solution.py:76
  16.2 2.1 %collective-permute-start.3 = (bf16[64,1280]{1,0:T(8,128)(2,1)S(1)}, bf16[64,1280]{1,0:T(8,128)(2,1)S(1)}, u32[]{:S(2)}, u32[]{:S(2)}) collective-permute-start(bf16[64,1280]{1,0:T(8,128)(2,1)S(1)} %constant_dynamic-update-slice_fusion.a0), channel_id=1, source_target_pairs={{0,4},{1,5},{2,6},{3,7},{4,0},{5,1},{6,2},{7,3},{8,12},{9,13},{10,... | collective-permute-start | bytes 491528 | tf_op jit(solution)/shard_map/ppermute | solution.py:76
  19.0 3.0 %copy-done.1 = bf16[3,3072,384]{2,1,0:T(8,128)(2,1)S(1)} copy-done((bf16[3,3072,384]{2,1,0:T(8,128)(2,1)S(1)}, bf16[3,3072,384]{2,1,0:T(8,128)(2,1)}, u32[]{:S(2)}) %copy-start.1) | copy-done | bytes 7077912
  22.5 1.9 %collective-permute-done.3.a3 = bf16[64,1280]{1,0:T(8,128)(2,1)S(1)} collective-permute-done((bf16[64,1280]{1,0:T(8,128)(2,1)S(1)}, bf16[64,1280]{1,0:T(8,128)(2,1)S(1)}, u32[]{:S(2)}, u32[]{:S(2)}) %collective-permute-start.3) | collective-permute-done | bytes 163872 | tf_op jit(solution)/shard_map/ppermute | solution.py:76
  24.5 1.8 %shard_map.196 = (bf16[2,256,384]{2,1,0:T(8,128)(2,1)S(1)}, bf16[256,3072]{1,0:T(8,128)(2,1)S(1)}) custom-call(bf16[64,1280]{1,0:T(8,128)(2,1)S(1)} %constant_dynamic-update-slice_fusion.a0, bf16[64,1280]{1,0:T(8,128)(2,1)S(1)} %collective-permute-done.1.a1, bf16[64,1280]{1,0:T(8,128)(2,1)S(1)} %collective-permute-done.2.a2, ...), custom_call_target="tpu_custom_call" | custom-call | tf_op jit(solution)/shard_map/pallas_call | solution.py:206
  26.4 2.0 %collective-permute-start.11 = (bf16[2,256,384]{2,1,0:T(8,128)(2,1)S(1)}, bf16[2,256,384]{2,1,0:T(8,128)(2,1)S(1)}, u32[]{:S(2)}, u32[]{:S(2)}) collective-permute-start(bf16[2,256,384]{2,1,0:T(8,128)(2,1)S(1)} %get-tuple-element.43.refs_1_), channel_id=1, source_target_pairs={{0,16},{8,120},{16,32},{24,8},{32,48},{40,24},{48,64},{56,40},{64,... | collective-permute-start | bytes 1179656 | tf_op jit(solution)/shard_map/ppermute | solution.py:72
  28.4 1.5 %shard_map.197 = bf16[256,384]{1,0:T(8,128)(2,1)S(1)} custom-call(bf16[256,3072]{1,0:T(8,128)(2,1)S(1)} %get-tuple-element.44.gathered, bf16[3072,384]{1,0:T(8,128)(2,1)S(1)} %get-tuple-element.45.weight, f32[1,128]{1,0:T(1,128)S(1)} %bitcast.27, f32[256,128]{1,0:T(8,128)S(1)} %get-tuple-element.112.cosine, f32[256,128]{1,0:T(8,128)S(1)} %get-tuple-element.111.sine), custom_call_target="tpu_custom_call" | custom-call | tf_op jit(solution)/shard_map/pallas_call | solution.py:222
  31.0 1.9 %collective-permute-start.14 = (bf16[2,256,384]{2,1,0:T(8,128)(2,1)S(1)}, bf16[2,256,384]{2,1,0:T(8,128)(2,1)S(1)}, u32[]{:S(2)}, u32[]{:S(2)}) collective-permute-start(bf16[2,256,384]{2,1,0:T(8,128)(2,1)S(1)} %collective-permute-done.8), channel_id=1, source_target_pairs={{0,16},{8,120},{16,32},{24,8},{32,48},{40,24},{48,64},{56,40},{64,... | collective-permute-start | bytes 1179656 | tf_op jit(solution)/shard_map/ppermute | solution.py:72
  33.0 5.1 %collective-permute-done.11.refs_2_ = bf16[2,256,384]{2,1,0:T(8,128)(2,1)S(1)} collective-permute-done((bf16[2,256,384]{2,1,0:T(8,128)(2,1)S(1)}, bf16[2,256,384]{2,1,0:T(8,128)(2,1)S(1)}, u32[]{:S(2)}, u32[]{:S(2)}) %collective-permute-start.11) | collective-permute-done | bytes 393248 | tf_op jit(solution)/shard_map/ppermute | solution.py:72
  38.8 2.3 %collective-permute-start.10 = (bf16[512,384]{1,0:T(8,128)(2,1)S(1)}, bf16[512,384]{1,0:T(8,128)(2,1)S(1)}, u32[]{:S(2)}, u32[]{:S(2)}) collective-permute-start(bf16[512,384]{1,0:T(8,128)(2,1)S(1)} %pad_maximum_fusion.1), channel_id=1, source_target_pairs={{0,8},{8,0},{16,24},{24,16},{32,40},{40,32},{48,56},{56,48},{64,72... | collective-permute-start | bytes 1179656 | tf_op jit(solution)/shard_map/ppermute | solution.py:68
  42.4 4.7 %collective-permute-done.12.refs_1_ = bf16[2,256,384]{2,1,0:T(8,128)(2,1)S(1)} collective-permute-done((bf16[2,256,384]{2,1,0:T(8,128)(2,1)S(1)}, bf16[2,256,384]{2,1,0:T(8,128)(2,1)S(1)}, u32[]{:S(2)}, u32[]{:S(2)}) %collective-permute-start.12) | collective-permute-done | bytes 393248 | tf_op jit(solution)/shard_map/ppermute | solution.py:72
  47.1 3.6 %shard_map.198 = (f32[384,1024]{1,0:T(8,128)S(1)}, f32[8,1024]{1,0:T(8,128)S(1)}) custom-call(bf16[1024,384]{1,0:T(8,128)(2,1)S(1)} %pad_maximum_fusion.refs_0_, bf16[2,256,384]{2,1,0:T(8,128)(2,1)S(1)} %get-tuple-element.43.refs_1_, bf16[2,256,384]{2,1,0:T(8,128)(2,1)S(1)} %collective-permute-done.11.refs_2_, ...), custom_call_target="tpu_custom_call" | custom-call | tf_op jit(solution)/shard_map/pallas_call | solution.py:308
  51.3 4.7 %collective-permute-done.13.refs_1_ = bf16[2,256,384]{2,1,0:T(8,128)(2,1)S(1)} collective-permute-done((bf16[2,256,384]{2,1,0:T(8,128)(2,1)S(1)}, bf16[2,256,384]{2,1,0:T(8,128)(2,1)S(1)}, u32[]{:S(2)}, u32[]{:S(2)}) %collective-permute-start.13) | collective-permute-done | bytes 393248 | tf_op jit(solution)/shard_map/ppermute | solution.py:72
  56.0 2.5 %shard_map.199 = (f32[384,1024]{1,0:T(8,128)S(1)}, f32[8,1024]{1,0:T(8,128)S(1)}) custom-call(bf16[1024,384]{1,0:T(8,128)(2,1)S(1)} %pad_maximum_fusion.refs_0_, bf16[2,256,384]{2,1,0:T(8,128)(2,1)S(1)} %collective-permute-done.12.refs_1_, bf16[2,256,384]{2,1,0:T(8,128)(2,1)S(1)} %collective-permute-done.16.refs_2_, ...), custom_call_target="tpu_custom_call" | custom-call | tf_op jit(solution)/shard_map/pallas_call | solution.py:308
  58.6 1.7 %collective-permute-done.17.refs_2_ = bf16[2,256,384]{2,1,0:T(8,128)(2,1)S(1)} collective-permute-done((bf16[2,256,384]{2,1,0:T(8,128)(2,1)S(1)}, bf16[2,256,384]{2,1,0:T(8,128)(2,1)S(1)}, u32[]{:S(2)}, u32[]{:S(2)}) %collective-permute-start.17) | collective-permute-done | bytes 393248 | tf_op jit(solution)/shard_map/ppermute | solution.py:72
  60.3 2.5 %shard_map.200 = (f32[384,1024]{1,0:T(8,128)S(1)}, f32[8,1024]{1,0:T(8,128)S(1)}) custom-call(bf16[1024,384]{1,0:T(8,128)(2,1)S(1)} %pad_maximum_fusion.refs_0_, bf16[2,256,384]{2,1,0:T(8,128)(2,1)S(1)} %collective-permute-done.13.refs_1_, bf16[2,256,384]{2,1,0:T(8,128)(2,1)S(1)} %collective-permute-done.17.refs_2_, ...), custom_call_target="tpu_custom_call" | custom-call | tf_op jit(solution)/shard_map/pallas_call | solution.py:308
  62.9 2.1 %collective-permute-done.15.refs_1_ = bf16[2,256,384]{2,1,0:T(8,128)(2,1)S(1)} collective-permute-done((bf16[2,256,384]{2,1,0:T(8,128)(2,1)S(1)}, bf16[2,256,384]{2,1,0:T(8,128)(2,1)S(1)}, u32[]{:S(2)}, u32[]{:S(2)}) %collective-permute-start.15) | collective-permute-done | bytes 393248 | tf_op jit(solution)/shard_map/ppermute | solution.py:72
  69.5 1.4 %collective-permute-start.20 = (bf16[400,128]{1,0:T(8,128)(2,1)S(1)}, bf16[400,128]{1,0:T(8,128)(2,1)S(1)}, u32[]{:S(2)}, u32[]{:S(2)}) collective-permute-start(bf16[400,128]{1,0:T(8,128)(2,1)S(1)} %get-tuple-element.58), channel_id=1, source_target_pairs={{0,128},{8,136},{16,144},{24,152},{32,160},{40,168},{48,176},{56,1... | collective-permute-start | bytes 307208 | tf_op jit(solution)/shard_map/ppermute | solution.py:68
  70.9 2.9 %collective-permute-start.22 = (bf16[400,128]{1,0:T(8,128)(2,1)S(1)}, bf16[400,128]{1,0:T(8,128)(2,1)S(1)}, u32[]{:S(2)}, u32[]{:S(2)}) collective-permute-start(bf16[400,128]{1,0:T(8,128)(2,1)S(1)} %get-tuple-element.62), channel_id=1, source_target_pairs={{0,130},{1,131},{2,128},{3,129},{4,134},{5,135},{6,132},{7,133},{8... | collective-permute-start | bytes 307208 | tf_op jit(solution)/shard_map/ppermute | solution.py:91
  75.7 2.3 %collective-permute-done.22.beyond = bf16[400,128]{1,0:T(8,128)(2,1)S(1)} collective-permute-done((bf16[400,128]{1,0:T(8,128)(2,1)S(1)}, bf16[400,128]{1,0:T(8,128)(2,1)S(1)}, u32[]{:S(2)}, u32[]{:S(2)}) %collective-permute-start.22) | collective-permute-done | bytes 102432 | tf_op jit(solution)/shard_map/ppermute | solution.py:91
  79.1 2.3 %collective-permute-start.24 = (bf16[32,3072]{1,0:T(8,128)(2,1)S(1)}, bf16[32,3072]{1,0:T(8,128)(2,1)S(1)}, u32[]{:S(2)}, u32[]{:S(2)}) collective-permute-start(bf16[32,3072]{1,0:T(8,128)(2,1)S(1)} %get-tuple-element.65), channel_id=1, source_target_pairs={{0,7},{1,6},{2,5},{3,4},{4,3},{5,2},{6,1},{7,0},{8,15},{9,14},{10,... | collective-permute-start | bytes 589832 | tf_op jit(solution)/shard_map/ppermute | solution.py:76
  81.3 1.7 %collective-permute-start.25 = (bf16[32,3072]{1,0:T(8,128)(2,1)S(1)}, bf16[32,3072]{1,0:T(8,128)(2,1)S(1)}, u32[]{:S(2)}, u32[]{:S(2)}) collective-permute-start(bf16[32,3072]{1,0:T(8,128)(2,1)S(1)} %get-tuple-element.66), channel_id=1, source_target_pairs={{0,6},{1,7},{2,4},{3,5},{4,2},{5,3},{6,0},{7,1},{8,14},{9,15},{10,... | collective-permute-start | bytes 589832 | tf_op jit(solution)/shard_map/ppermute | solution.py:76
  84.2 4.6 %collective-permute-done.24.a = bf16[32,3072]{1,0:T(8,128)(2,1)S(1)} collective-permute-done((bf16[32,3072]{1,0:T(8,128)(2,1)S(1)}, bf16[32,3072]{1,0:T(8,128)(2,1)S(1)}, u32[]{:S(2)}, u32[]{:S(2)}) %collective-permute-start.24) | collective-permute-done | bytes 196640 | tf_op jit(solution)/shard_map/ppermute | solution.py:76
  88.8 1.9 %collective-permute-done.25.b = bf16[32,3072]{1,0:T(8,128)(2,1)S(1)} collective-permute-done((bf16[32,3072]{1,0:T(8,128)(2,1)S(1)}, bf16[32,3072]{1,0:T(8,128)(2,1)S(1)}, u32[]{:S(2)}, u32[]{:S(2)}) %collective-permute-start.25) | collective-permute-done | bytes 196640 | tf_op jit(solution)/shard_map/ppermute | solution.py:76
  92.6 5.9 %collective-permute-start.28 = (bf16[2,1,16,16]{3,2,1,0:T(8,128)(2,1)S(1)}, bf16[2,1,16,16]{3,2,1,0:T(8,128)(2,1)S(1)}, u32[]{:S(2)}, u32[]{:S(2)}) collective-permute-start(bf16[2,1,16,16]{3,2,1,0:T(8,128)(2,1)S(1)} %get-tuple-element.107), channel_id=1, source_target_pairs={{8,16},{24,32},{40,48},{56,64},{72,80},{88,96},{104,112},{120,128}... | collective-permute-start | bytes 3080 | tf_op jit(solution)/shard_map/ppermute | solution.py:447
  98.5 2.7 %collective-permute-done.28 = bf16[2,1,16,16]{3,2,1,0:T(8,128)(2,1)S(1)} collective-permute-done((bf16[2,1,16,16]{3,2,1,0:T(8,128)(2,1)S(1)}, bf16[2,1,16,16]{3,2,1,0:T(8,128)(2,1)S(1)}, u32[]{:S(2)}, u32[]{:S(2)}) %collective-permute-start.28) | collective-permute-done | bytes 1056 | tf_op jit(solution)/shard_map/ppermute | solution.py:447
  101.2 1.4 %collective-permute-start.29 = (bf16[2,6,1,16]{3,2,1,0:T(2,128)(2,1)S(1)}, bf16[2,6,1,16]{3,2,1,0:T(2,128)(2,1)S(1)}, u32[]{:S(2)}, u32[]{:S(2)}) collective-permute-start(bf16[2,6,1,16]{3,2,1,0:T(2,128)(2,1)S(1)} %broadcast_select_fusion.4), channel_id=1, source_target_pairs={{0,1},{1,0},{2,3},{3,2},{4,5},{5,4},{6,7},{7,6},{8,9},{9,8},{10,11... | collective-permute-start | bytes 1160 | tf_op jit(solution)/shard_map/ppermute | solution.py:445
  102.6 2.3 %collective-permute-start.30 = (bf16[2,6,1,16]{3,2,1,0:T(2,128)(2,1)S(1)}, bf16[2,6,1,16]{3,2,1,0:T(2,128)(2,1)S(1)}, u32[]{:S(2)}, u32[]{:S(2)}) collective-permute-start(bf16[2,6,1,16]{3,2,1,0:T(2,128)(2,1)S(1)} %get-tuple-element.74), channel_id=1, source_target_pairs={{1,2},{3,4},{5,6},{2,1},{4,3},{6,5},{9,10},{11,12},{13,14},{10,9},... | collective-permute-start | bytes 1160 | tf_op jit(solution)/shard_map/ppermute | solution.py:447
  104.9 4.0 %collective-permute-done.30 = bf16[2,6,1,16]{3,2,1,0:T(2,128)(2,1)S(1)} collective-permute-done((bf16[2,6,1,16]{3,2,1,0:T(2,128)(2,1)S(1)}, bf16[2,6,1,16]{3,2,1,0:T(2,128)(2,1)S(1)}, u32[]{:S(2)}, u32[]{:S(2)}) %collective-permute-start.30) | collective-permute-done | bytes 416 | tf_op jit(solution)/shard_map/ppermute | solution.py:447
  (109 shorter events, 23.6 us)
Async XLA Ops:
  0.6 109.0 %copy-start = (bf16[3,3,3,16,512]{4,3,2,1,0:T(8,128)(2,1)S(1)}, bf16[3,3,3,16,512]{4,3,2,1,0:T(8,128)(2,1)}, u32[]{:S(2)}) copy-start(bf16[3,3,3,16,512]{4,3,2,1,0:T(8,128)(2,1)} %param.31) | copy-start | bytes 1327108
  2.7 7.0 %collective-permute-start.4 = (bf16[32,1792]{1,0:T(8,128)(2,1)S(1)}, bf16[32,1792]{1,0:T(8,128)(2,1)S(1)}, u32[]{:S(2)}, u32[]{:S(2)}) collective-permute-start(bf16[32,1792]{1,0:T(8,128)(2,1)S(1)} %get-tuple-element.39), channel_id=1, source_target_pairs={{0,6},{1,7},{2,4},{3,5},{4,2},{5,3},{6,0},{7,1},{8,14},{9,15},{10,... | collective-permute-start | bytes 344072 | tf_op jit(solution)/shard_map/ppermute | solution.py:76
  5.6 5.8 %collective-permute-start.5 = (bf16[32,1792]{1,0:T(8,128)(2,1)S(1)}, bf16[32,1792]{1,0:T(8,128)(2,1)S(1)}, u32[]{:S(2)}, u32[]{:S(2)}) collective-permute-start(bf16[32,1792]{1,0:T(8,128)(2,1)S(1)} %get-tuple-element.39), channel_id=1, source_target_pairs={{0,2},{1,3},{2,0},{3,1},{4,6},{5,7},{6,4},{7,5},{8,10},{9,11},{10,... | collective-permute-start | bytes 344072 | tf_op jit(solution)/shard_map/ppermute | solution.py:76
  5.8 6.9 %collective-permute-start.6 = (bf16[32,1792]{1,0:T(8,128)(2,1)S(1)}, bf16[32,1792]{1,0:T(8,128)(2,1)S(1)}, u32[]{:S(2)}, u32[]{:S(2)}) collective-permute-start(bf16[32,1792]{1,0:T(8,128)(2,1)S(1)} %get-tuple-element.39), channel_id=1, source_target_pairs={{0,4},{1,5},{2,6},{3,7},{4,0},{5,1},{6,2},{7,3},{8,12},{9,13},{10,... | collective-permute-start | bytes 344072 | tf_op jit(solution)/shard_map/ppermute | solution.py:76
  7.5 6.1 %collective-permute-start = (bf16[32,1280]{1,0:T(8,128)(2,1)S(1)}, bf16[32,1280]{1,0:T(8,128)(2,1)S(1)}, u32[]{:S(2)}, u32[]{:S(2)}) collective-permute-start(bf16[32,1280]{1,0:T(8,128)(2,1)S(1)} %get-tuple-element.38), channel_id=1, source_target_pairs={{0,1},{1,0},{2,3},{3,2},{4,5},{5,4},{6,7},{7,6},{8,9},{9,8},{10,11... | collective-permute-start | bytes 245768 | tf_op jit(solution)/shard_map/ppermute | solution.py:76
  12.7 11.7 %collective-permute-start.7 = (bf16[128,1792]{1,0:T(8,128)(2,1)S(1)}, bf16[128,1792]{1,0:T(8,128)(2,1)S(1)}, u32[]{:S(2)}, u32[]{:S(2)}) collective-permute-start(bf16[128,1792]{1,0:T(8,128)(2,1)S(1)} %constant_dynamic-update-slice_fusion.2.b0), channel_id=1, source_target_pairs={{0,1},{1,0},{2,3},{3,2},{4,5},{5,4},{6,7},{7,6},{8,9},{9,8},{10,11... | collective-permute-start | bytes 1376264 | tf_op jit(solution)/shard_map/ppermute | solution.py:76
  13.6 8.9 %collective-permute-start.1 = (bf16[64,1280]{1,0:T(8,128)(2,1)S(1)}, bf16[64,1280]{1,0:T(8,128)(2,1)S(1)}, u32[]{:S(2)}, u32[]{:S(2)}) collective-permute-start(bf16[64,1280]{1,0:T(8,128)(2,1)S(1)} %constant_dynamic-update-slice_fusion.a0), channel_id=1, source_target_pairs={{0,6},{1,7},{2,4},{3,5},{4,2},{5,3},{6,0},{7,1},{8,14},{9,15},{10,... | collective-permute-start | bytes 491528 | tf_op jit(solution)/shard_map/ppermute | solution.py:76
  16.2 6.3 %collective-permute-start.2 = (bf16[64,1280]{1,0:T(8,128)(2,1)S(1)}, bf16[64,1280]{1,0:T(8,128)(2,1)S(1)}, u32[]{:S(2)}, u32[]{:S(2)}) collective-permute-start(bf16[64,1280]{1,0:T(8,128)(2,1)S(1)} %constant_dynamic-update-slice_fusion.a0), channel_id=1, source_target_pairs={{0,2},{1,3},{2,0},{3,1},{4,6},{5,7},{6,4},{7,5},{8,10},{9,11},{10,... | collective-permute-start | bytes 491528 | tf_op jit(solution)/shard_map/ppermute | solution.py:76
  16.2 8.2 %collective-permute-start.3 = (bf16[64,1280]{1,0:T(8,128)(2,1)S(1)}, bf16[64,1280]{1,0:T(8,128)(2,1)S(1)}, u32[]{:S(2)}, u32[]{:S(2)}) collective-permute-start(bf16[64,1280]{1,0:T(8,128)(2,1)S(1)} %constant_dynamic-update-slice_fusion.a0), channel_id=1, source_target_pairs={{0,4},{1,5},{2,6},{3,7},{4,0},{5,1},{6,2},{7,3},{8,12},{9,13},{10,... | collective-permute-start | bytes 491528 | tf_op jit(solution)/shard_map/ppermute | solution.py:76
  26.3 2.1 %collective-permute-start.8 = (bf16[2,256,384]{2,1,0:T(8,128)(2,1)S(1)}, bf16[2,256,384]{2,1,0:T(8,128)(2,1)S(1)}, u32[]{:S(2)}, u32[]{:S(2)}) collective-permute-start(bf16[2,256,384]{2,1,0:T(8,128)(2,1)S(1)} %get-tuple-element.43.refs_1_), channel_id=1, source_target_pairs={{0,8},{8,0},{16,24},{24,16},{32,40},{40,32},{48,56},{56,48},{64,72... | collective-permute-start | bytes 1179656 | tf_op jit(solution)/shard_map/ppermute | solution.py:68
  26.4 11.7 %collective-permute-start.11 = (bf16[2,256,384]{2,1,0:T(8,128)(2,1)S(1)}, bf16[2,256,384]{2,1,0:T(8,128)(2,1)S(1)}, u32[]{:S(2)}, u32[]{:S(2)}) collective-permute-start(bf16[2,256,384]{2,1,0:T(8,128)(2,1)S(1)} %get-tuple-element.43.refs_1_), channel_id=1, source_target_pairs={{0,16},{8,120},{16,32},{24,8},{32,48},{40,24},{48,64},{56,40},{64,... | collective-permute-start | bytes 1179656 | tf_op jit(solution)/shard_map/ppermute | solution.py:72
  29.9 8.9 %collective-permute-start.9 = (bf16[256,384]{1,0:T(8,128)(2,1)S(1)}, bf16[256,384]{1,0:T(8,128)(2,1)S(1)}, u32[]{:S(2)}, u32[]{:S(2)}) collective-permute-start(bf16[256,384]{1,0:T(8,128)(2,1)S(1)} %shard_map.197), channel_id=1, source_target_pairs={{0,128},{8,136},{16,144},{24,152},{32,160},{40,168},{48,176},{56,1... | collective-permute-start | bytes 589832 | tf_op jit(solution)/shard_map/ppermute | solution.py:68
  31.0 11.3 %collective-permute-start.14 = (bf16[2,256,384]{2,1,0:T(8,128)(2,1)S(1)}, bf16[2,256,384]{2,1,0:T(8,128)(2,1)S(1)}, u32[]{:S(2)}, u32[]{:S(2)}) collective-permute-start(bf16[2,256,384]{2,1,0:T(8,128)(2,1)S(1)} %collective-permute-done.8), channel_id=1, source_target_pairs={{0,16},{8,120},{16,32},{24,8},{32,48},{40,24},{48,64},{56,40},{64,... | collective-permute-start | bytes 1179656 | tf_op jit(solution)/shard_map/ppermute | solution.py:72
  38.1 9.0 %collective-permute-start.12 = (bf16[2,256,384]{2,1,0:T(8,128)(2,1)S(1)}, bf16[2,256,384]{2,1,0:T(8,128)(2,1)S(1)}, u32[]{:S(2)}, u32[]{:S(2)}) collective-permute-start(bf16[2,256,384]{2,1,0:T(8,128)(2,1)S(1)} %collective-permute-done.11.refs_2_), channel_id=1, source_target_pairs={{0,16},{8,120},{16,32},{24,8},{32,48},{40,24},{48,64},{56,40},{64,... | collective-permute-start | bytes 1179656 | tf_op jit(solution)/shard_map/ppermute | solution.py:72
  38.1 27.8 %collective-permute-start.18 = (bf16[192,3072]{1,0:T(8,128)(2,1)S(1)}, bf16[192,3072]{1,0:T(8,128)(2,1)S(1)}, u32[]{:S(2)}, u32[]{:S(2)}) collective-permute-start(bf16[192,3072]{1,0:T(8,128)(2,1)S(1)} %constant_dynamic-slice_fusion), channel_id=1, source_target_pairs={{0,2},{1,3},{2,0},{3,1},{4,6},{5,7},{6,4},{7,5},{8,10},{9,11},{10,... | collective-permute-start | bytes 3538952 | tf_op jit(solution)/shard_map/ppermute | solution.py:76
  38.8 8.3 %collective-permute-start.10 = (bf16[512,384]{1,0:T(8,128)(2,1)S(1)}, bf16[512,384]{1,0:T(8,128)(2,1)S(1)}, u32[]{:S(2)}, u32[]{:S(2)}) collective-permute-start(bf16[512,384]{1,0:T(8,128)(2,1)S(1)} %pad_maximum_fusion.1), channel_id=1, source_target_pairs={{0,8},{8,0},{16,24},{24,16},{32,40},{40,32},{48,56},{56,48},{64,72... | collective-permute-start | bytes 1179656 | tf_op jit(solution)/shard_map/ppermute | solution.py:68
  42.4 9.0 %collective-permute-start.16 = (bf16[2,256,384]{2,1,0:T(8,128)(2,1)S(1)}, bf16[2,256,384]{2,1,0:T(8,128)(2,1)S(1)}, u32[]{:S(2)}, u32[]{:S(2)}) collective-permute-start(bf16[2,256,384]{2,1,0:T(8,128)(2,1)S(1)} %collective-permute-done.14.refs_3_), channel_id=1, source_target_pairs={{0,16},{8,120},{16,32},{24,8},{32,48},{40,24},{48,64},{56,40},{64,... | collective-permute-start | bytes 1179656 | tf_op jit(solution)/shard_map/ppermute | solution.py:72
  47.1 9.0 %collective-permute-start.13 = (bf16[2,256,384]{2,1,0:T(8,128)(2,1)S(1)}, bf16[2,256,384]{2,1,0:T(8,128)(2,1)S(1)}, u32[]{:S(2)}, u32[]{:S(2)}) collective-permute-start(bf16[2,256,384]{2,1,0:T(8,128)(2,1)S(1)} %collective-permute-done.12.refs_1_), channel_id=1, source_target_pairs={{0,16},{8,120},{16,32},{24,8},{32,48},{40,24},{48,64},{56,40},{64,... | collective-permute-start | bytes 1179656 | tf_op jit(solution)/shard_map/ppermute | solution.py:72
  51.3 9.0 %collective-permute-start.17 = (bf16[2,256,384]{2,1,0:T(8,128)(2,1)S(1)}, bf16[2,256,384]{2,1,0:T(8,128)(2,1)S(1)}, u32[]{:S(2)}, u32[]{:S(2)}) collective-permute-start(bf16[2,256,384]{2,1,0:T(8,128)(2,1)S(1)} %collective-permute-done.16.refs_2_), channel_id=1, source_target_pairs={{0,16},{8,120},{16,32},{24,8},{32,48},{40,24},{48,64},{56,40},{64,... | collective-permute-start | bytes 1179656 | tf_op jit(solution)/shard_map/ppermute | solution.py:72
  56.0 9.0 %collective-permute-start.15 = (bf16[2,256,384]{2,1,0:T(8,128)(2,1)S(1)}, bf16[2,256,384]{2,1,0:T(8,128)(2,1)S(1)}, u32[]{:S(2)}, u32[]{:S(2)}) collective-permute-start(bf16[2,256,384]{2,1,0:T(8,128)(2,1)S(1)} %collective-permute-done.13.refs_1_), channel_id=1, source_target_pairs={{0,16},{8,120},{16,32},{24,8},{32,48},{40,24},{48,64},{56,40},{64,... | collective-permute-start | bytes 1179656 | tf_op jit(solution)/shard_map/ppermute | solution.py:72
  65.9 2.2 %collective-permute-start.19 = (bf16[400,512]{1,0:T(8,128)(2,1)S(1)}, bf16[400,512]{1,0:T(8,128)(2,1)S(1)}, u32[]{:S(2)}, u32[]{:S(2)}) collective-permute-start(bf16[400,512]{1,0:T(8,128)(2,1)S(1)} %shard_map.202), channel_id=1, source_target_pairs={{0,8},{8,0},{16,24},{24,16},{32,40},{40,32},{48,56},{56,48},{64,72... | collective-permute-start | bytes 1228808 | tf_op jit(solution)/shard_map/ppermute | solution.py:68
  68.4 5.5 %collective-permute-start.23 = (bf16[192,3072]{1,0:T(8,128)(2,1)S(1)}, bf16[192,3072]{1,0:T(8,128)(2,1)S(1)}, u32[]{:S(2)}, u32[]{:S(2)}) collective-permute-start(bf16[192,3072]{1,0:T(8,128)(2,1)S(1)} %collective-permute-done.18), channel_id=1, source_target_pairs={{0,8},{8,0},{16,24},{24,16},{32,40},{40,32},{48,56},{56,48},{64,72... | collective-permute-start | bytes 3538952 | tf_op jit(solution)/shard_map/ppermute | solution.py:68
  68.8 5.9 %collective-permute-start.21 = (bf16[400,128]{1,0:T(8,128)(2,1)S(1)}, bf16[400,128]{1,0:T(8,128)(2,1)S(1)}, u32[]{:S(2)}, u32[]{:S(2)}) collective-permute-start(bf16[400,128]{1,0:T(8,128)(2,1)S(1)} %get-tuple-element.61), channel_id=1, source_target_pairs={{0,2},{1,3},{2,0},{3,1},{4,6},{5,7},{6,4},{7,5},{8,10},{9,11},{10,... | collective-permute-start | bytes 307208 | tf_op jit(solution)/shard_map/ppermute | solution.py:76
  69.5 6.2 %collective-permute-start.20 = (bf16[400,128]{1,0:T(8,128)(2,1)S(1)}, bf16[400,128]{1,0:T(8,128)(2,1)S(1)}, u32[]{:S(2)}, u32[]{:S(2)}) collective-permute-start(bf16[400,128]{1,0:T(8,128)(2,1)S(1)} %get-tuple-element.58), channel_id=1, source_target_pairs={{0,128},{8,136},{16,144},{24,152},{32,160},{40,168},{48,176},{56,1... | collective-permute-start | bytes 307208 | tf_op jit(solution)/shard_map/ppermute | solution.py:68
  70.9 7.1 %collective-permute-start.22 = (bf16[400,128]{1,0:T(8,128)(2,1)S(1)}, bf16[400,128]{1,0:T(8,128)(2,1)S(1)}, u32[]{:S(2)}, u32[]{:S(2)}) collective-permute-start(bf16[400,128]{1,0:T(8,128)(2,1)S(1)} %get-tuple-element.62), channel_id=1, source_target_pairs={{0,130},{1,131},{2,128},{3,129},{4,134},{5,135},{6,132},{7,133},{8... | collective-permute-start | bytes 307208 | tf_op jit(solution)/shard_map/ppermute | solution.py:91
  79.1 9.8 %collective-permute-start.24 = (bf16[32,3072]{1,0:T(8,128)(2,1)S(1)}, bf16[32,3072]{1,0:T(8,128)(2,1)S(1)}, u32[]{:S(2)}, u32[]{:S(2)}) collective-permute-start(bf16[32,3072]{1,0:T(8,128)(2,1)S(1)} %get-tuple-element.65), channel_id=1, source_target_pairs={{0,7},{1,6},{2,5},{3,4},{4,3},{5,2},{6,1},{7,0},{8,15},{9,14},{10,... | collective-permute-start | bytes 589832 | tf_op jit(solution)/shard_map/ppermute | solution.py:76
  81.3 9.4 %collective-permute-start.25 = (bf16[32,3072]{1,0:T(8,128)(2,1)S(1)}, bf16[32,3072]{1,0:T(8,128)(2,1)S(1)}, u32[]{:S(2)}, u32[]{:S(2)}) collective-permute-start(bf16[32,3072]{1,0:T(8,128)(2,1)S(1)} %get-tuple-element.66), channel_id=1, source_target_pairs={{0,6},{1,7},{2,4},{3,5},{4,2},{5,3},{6,0},{7,1},{8,14},{9,15},{10,... | collective-permute-start | bytes 589832 | tf_op jit(solution)/shard_map/ppermute | solution.py:76
  83.1 7.8 %collective-permute-start.26 = (bf16[32,3072]{1,0:T(8,128)(2,1)S(1)}, bf16[32,3072]{1,0:T(8,128)(2,1)S(1)}, u32[]{:S(2)}, u32[]{:S(2)}) collective-permute-start(bf16[32,3072]{1,0:T(8,128)(2,1)S(1)} %get-tuple-element.67), channel_id=1, source_target_pairs={{0,1},{1,0},{2,3},{3,2},{4,5},{5,4},{6,7},{7,6},{8,9},{9,8},{10,11... | collective-permute-start | bytes 589832 | tf_op jit(solution)/shard_map/ppermute | solution.py:76
  92.5 6.0 %collective-permute-start.27 = (bf16[2,1,16,16]{3,2,1,0:T(8,128)(2,1)S(1)}, bf16[2,1,16,16]{3,2,1,0:T(8,128)(2,1)S(1)}, u32[]{:S(2)}, u32[]{:S(2)}) collective-permute-start(bf16[2,1,16,16]{3,2,1,0:T(8,128)(2,1)S(1)} %get-tuple-element.108), channel_id=1, source_target_pairs={{0,8},{8,0},{16,24},{24,16},{32,40},{40,32},{48,56},{56,48},{64,72... | collective-permute-start | bytes 3080 | tf_op jit(solution)/shard_map/ppermute | solution.py:445
  92.6 8.6 %collective-permute-start.28 = (bf16[2,1,16,16]{3,2,1,0:T(8,128)(2,1)S(1)}, bf16[2,1,16,16]{3,2,1,0:T(8,128)(2,1)S(1)}, u32[]{:S(2)}, u32[]{:S(2)}) collective-permute-start(bf16[2,1,16,16]{3,2,1,0:T(8,128)(2,1)S(1)} %get-tuple-element.107), channel_id=1, source_target_pairs={{8,16},{24,32},{40,48},{56,64},{72,80},{88,96},{104,112},{120,128}... | collective-permute-start | bytes 3080 | tf_op jit(solution)/shard_map/ppermute | solution.py:447
  101.2 3.7 %collective-permute-start.29 = (bf16[2,6,1,16]{3,2,1,0:T(2,128)(2,1)S(1)}, bf16[2,6,1,16]{3,2,1,0:T(2,128)(2,1)S(1)}, u32[]{:S(2)}, u32[]{:S(2)}) collective-permute-start(bf16[2,6,1,16]{3,2,1,0:T(2,128)(2,1)S(1)} %broadcast_select_fusion.4), channel_id=1, source_target_pairs={{0,1},{1,0},{2,3},{3,2},{4,5},{5,4},{6,7},{7,6},{8,9},{9,8},{10,11... | collective-permute-start | bytes 1160 | tf_op jit(solution)/shard_map/ppermute | solution.py:445
  102.6 6.4 %collective-permute-start.30 = (bf16[2,6,1,16]{3,2,1,0:T(2,128)(2,1)S(1)}, bf16[2,6,1,16]{3,2,1,0:T(2,128)(2,1)S(1)}, u32[]{:S(2)}, u32[]{:S(2)}) collective-permute-start(bf16[2,6,1,16]{3,2,1,0:T(2,128)(2,1)S(1)} %get-tuple-element.74), channel_id=1, source_target_pairs={{1,2},{3,4},{5,6},{2,1},{4,3},{6,5},{9,10},{11,12},{13,14},{10,9},... | collective-permute-start | bytes 1160 | tf_op jit(solution)/shard_map/ppermute | solution.py:447
  (16 other events, 177.6 us)
